TPU v7x, 32 devices: a whole 2x2x4 slice. The times are simulated.
32 devices in a mesh: batch: 4 (over y, x), seq: 8 (over z, core).
Axes of the slice: x: 2, y: 2, z: 4, core: 2. Of those that a mesh axis runs over, the one named last changes fastest.
Arguments:
- inputs: bfloat16 [4, 16384, 512], P('batch', 'seq'), may hold values from -6 to 6
- out_grad: bfloat16 [4, 16384, 512], P('batch', 'seq'), may hold values from -6 to 6
- lengths: int32 [4], P('batch'), may hold values from 128 to 16384, as said below
- qkv_weight: float32 [512, 1536], P(('batch', 'seq')), may hold values from -0.125 to 0.125
- proj_weight: float32 [512, 512], P(('batch', 'seq')), may hold values from -3 to 3
- up_weight: float32 [512, 2048], P(('batch', 'seq')), may hold values from -0.125 to 0.125
- down_weight: float32 [2048, 512], P(('batch', 'seq')), may hold values from -0.125 to 0.125
- norm_params: float32 [4, 512], P(None, ('batch', 'seq'))
- qkv_mean: float32 [512, 1536], P(('batch', 'seq')), may hold values from -0.0034179688 to 0.0034179688
- proj_mean: float32 [512, 512], P(('batch', 'seq')), may hold values from -0.0007324219 to 0.0007324219
- up_mean: float32 [512, 2048], P(('batch', 'seq')), may hold values from -0.0007324219 to 0.0007324219
- down_mean: float32 [2048, 512], P(('batch', 'seq')), may hold values from -0.0004272461 to 0.0004272461
- norm_mean: float32 [4, 512], P(None, ('batch', 'seq')), may hold values from -0.009765625 to 0.009765625
- qkv_second: float32 [512, 1536], P(('batch', 'seq')), may hold values from 3.1768462e-07 to 1.2707385e-06
- proj_second: float32 [512, 512], P(('batch', 'seq')), may hold values from 1.588423e-08 to 6.353692e-08
- up_second: float32 [512, 2048], P(('batch', 'seq')), may hold values from 1.588423e-08 to 6.353692e-08
- down_second: float32 [2048, 512], P(('batch', 'seq')), may hold values from 4.9638222e-09 to 1.9855289e-08
- norm_second: float32 [4, 512], P(None, ('batch', 'seq')), may hold values from 2.8591614e-06 to 1.1436646e-05
Outputs:
- outputs: bfloat16 [4, 16384, 512], P('batch', 'seq')
- input_grad: float32 [4, 16384, 512], P('batch', 'seq')
- grad_norm: float32 [], replicated
- qkv_moment: float32 [512, 1536], P(('batch', 'seq'))
- proj_moment: float32 [512, 512], P(('batch', 'seq'))
- up_moment: float32 [512, 2048], P(('batch', 'seq'))
- down_moment: float32 [2048, 512], P(('batch', 'seq'))
- norm_moment: float32 [4, 512], P(None, ('batch', 'seq'))
- qkv_square: float32 [512, 1536], P(('batch', 'seq'))
- proj_square: float32 [512, 512], P(('batch', 'seq'))
- up_square: float32 [512, 2048], P(('batch', 'seq'))
- down_square: float32 [2048, 512], P(('batch', 'seq'))
- norm_square: float32 [4, 512], P(None, ('batch', 'seq'))
- qkv_master: float32 [512, 1536], P(('batch', 'seq'))
- proj_master: float32 [512, 512], P(('batch', 'seq'))
- up_master: float32 [512, 2048], P(('batch', 'seq'))
- down_master: float32 [2048, 512], P(('batch', 'seq'))
- norm_master: float32 [4, 512], P(None, ('batch', 'seq'))
- shift_clipped: float32 [512], P(('batch', 'seq'))
Inputs may be any that keep to these rules, and one draw needn't show every extreme that they name: `lengths`: one of the 4 sequences in every draw has all 16384 tokens.
All inputs are finite; a program needn't handle non-finite values.
Results may differ from a plain program's by a relative error of at most 0.012.
The roundings to bfloat16 on the way count: a program that leaves them out, or rounds other values in their place, can miss the bound.
Values may be sent and summed in bfloat16 or wider, within the bound.
A program may use at most 384 MiB of HBM per device.

v0:
```python
import functools
import jax
import jax.numpy as jnp
from jax import lax
from jax.experimental import pallas as pl
from jax.experimental.pallas import tpu as pltpu
from jax.sharding import PartitionSpec as P

HEADS = 8
HD = 64
SPAN = 128
STEP = 10
LN_EPS = 1e-05
NEG_FILL = -1e30
CLIP = 1.0
BETA = 0.5
ADAM_EPS = 1e-08
DECAY = 0.1
RATES = (0.02, 0.3, 0.02, 0.02, 0.5)
BF = jnp.bfloat16
F32 = jnp.float32
LANES = 128
VMEM_LIMIT = 56 * 1024 * 1024


def dot(a, b, dims=((1,), (0,))):
    return lax.dot_general(a, b, (dims, ((), ())), preferred_element_type=F32)


def dot_tn(a, b):
    return dot(a, b, ((0,), (0,)))


def dot_nt(a, b):
    return dot(a, b, ((1,), (1,)))


def normalize(x):
    inv = 1.0 / x.shape[-1]
    centred = x - jnp.sum(x, axis=-1, keepdims=True) * inv
    spread = jnp.sum(centred * centred, axis=-1, keepdims=True) * inv
    rstd = lax.rsqrt(spread + LN_EPS)
    return centred * rstd, rstd


def norm_back(grad, gain, xhat, rstd):
    inv = 1.0 / grad.shape[-1]
    e = grad * gain
    mean_e = jnp.sum(e, axis=-1, keepdims=True) * inv
    mean_ex = jnp.sum(e * xhat, axis=-1, keepdims=True) * inv
    return rstd * (e - mean_e - xhat * mean_ex)


def qkv_tile(x, norms_ref, weight_ref):
    xhat, _ = normalize(x.astype(F32))
    normed = (xhat * norms_ref[0:1, :] + norms_ref[1:2, :]).astype(BF)
    return dot(normed, weight_ref[...]).astype(BF)


def span_scale(length, begin, shape):
    count = jnp.clip(length - begin, 1, SPAN)
    return lax.rsqrt(jnp.full(shape, count, jnp.int32).astype(F32))


def span_sum(kv, length, begin):
    row = lax.broadcasted_iota(jnp.int32, kv.shape, 0)
    kept = jnp.where(row < length - begin, kv.astype(F32), 0.0)
    total = jnp.sum(kept, axis=0, keepdims=True)
    return total * span_scale(length, begin, total.shape)


def stack_heads(pair):
    lane = lax.broadcasted_iota(jnp.int32, pair.shape, 1)
    zero = jnp.zeros_like(pair)
    return jnp.concatenate(
        [jnp.where(lane < HD, pair, zero), jnp.where(lane >= HD, pair, zero)], axis=0
    )


def fold_heads(both):
    picked = jnp.concatenate([both[:HD, :SPAN], both[HD:, SPAN:]], axis=0)
    return picked.T


def span_caps(length, span):
    query_pos = lax.broadcasted_iota(jnp.int32, (1, 2 * SPAN), 1) & (SPAN - 1)
    near_cap = jnp.minimum(query_pos, length - span * SPAN - 1)
    far_cap = jnp.minimum(span, (length + SPAN - 1) // SPAN)
    return near_cap, far_cap


def mask_scores(raw, caps):
    near_cap, far_cap = caps
    key_pos = lax.broadcasted_iota(jnp.int32, (SPAN, 2 * SPAN), 0)
    summ_pos = lax.broadcasted_iota(jnp.int32, (raw.shape[0] - SPAN, 2 * SPAN), 0)
    near = jnp.where(key_pos <= near_cap, raw[:SPAN], NEG_FILL)
    far = jnp.where(summ_pos < far_cap, raw[SPAN:], NEG_FILL)
    return jnp.concatenate([near, far], axis=0)


def attend_spans(spans, mixed_ref, width, summ_ref, summ_vt_ref, out_ref, lse_ref):
    units = [(pl.ds(row, SPAN), index, caps, pair) for row, index, caps in spans for pair in range(width // LANES)]
    queries, keys, values_t = [], [], []
    for rows, index, caps, pair in units:
        at = pair * LANES
        queries.append(stack_heads(mixed_ref[rows, at : at + LANES] * BF(0.125)))
        near_k = mixed_ref[rows, width + at : width + at + LANES]
        near_v = mixed_ref[rows, 2 * width + at : 2 * width + at + LANES]
        keys.append(jnp.concatenate([near_k, summ_ref[:, at : at + LANES]], axis=0))
        values_t.append(jnp.concatenate([near_v.T, summ_vt_ref[at : at + LANES, :]], axis=1))
    scores = [dot_nt(k, q) for k, q in zip(keys, queries)]
    scores = [mask_scores(s, unit[2]) for s, unit in zip(scores, units)]
    peaks = [jnp.max(s, axis=0, keepdims=True) for s in scores]
    expos = [jnp.exp(s - p) for s, p in zip(scores, peaks)]
    totals = [jnp.sum(e, axis=0, keepdims=True) for e in expos]
    expos = [e.astype(BF) for e in expos]
    outs = [dot(v, e) for v, e in zip(values_t, expos)]
    outs = [o * (1.0 / t) for o, t in zip(outs, totals)]
    for (rows, index, caps, pair), out, peak, total in zip(units, outs, peaks, totals):
        at = pair * LANES
        out_ref[rows, at : at + LANES] = fold_heads(out).astype(BF)
        lse_ref[index, pair : pair + 1, :] = peak + jnp.log(total)


def attend_back_spans(
    spans, mixed_ref, grad_ref, width, summ_ref, summ_kt_ref, lse_ref, back_ref, dsumm_ref
):
    pairs = width // LANES
    units = [(pl.ds(row, SPAN), index, caps, pair) for row, index, caps in spans for pair in range(pairs)]
    queries, grads, keys, keys_t, values = [], [], [], [], []
    for rows, index, caps, pair in units:
        at = pair * LANES
        queries.append(stack_heads(mixed_ref[rows, at : at + LANES] * BF(0.125)))
        grads.append(stack_heads(grad_ref[rows, at : at + LANES]))
        near_k = mixed_ref[rows, width + at : width + at + LANES]
        near_v = mixed_ref[rows, 2 * width + at : 2 * width + at + LANES]
        keys.append(jnp.concatenate([near_k, summ_ref[:, at : at + LANES]], axis=0))
        keys_t.append(jnp.concatenate([near_k.T, summ_kt_ref[at : at + LANES, :]], axis=1))
        values.append(jnp.concatenate([near_v, summ_ref[:, width + at : width + at + LANES]], axis=0))
    scores = [dot_nt(k, q) for k, q in zip(keys, queries)]
    dprobs = [dot_nt(v, g) for v, g in zip(values, grads)]
    scores = [mask_scores(s, unit[2]) for s, unit in zip(scores, units)]
    probs = [jnp.exp(s - lse_ref[index, pair : pair + 1, :]) for s, (_, index, _, pair) in zip(scores, units)]
    deltas = [jnp.sum(p * d, axis=0, keepdims=True) for p, d in zip(probs, dprobs)]
    dscores = [(p * (d - delta)).astype(BF) for p, d, delta in zip(probs, dprobs, deltas)]
    probs = [p.astype(BF) for p in probs]
    dqs = [dot(k, ds) for k, ds in zip(keys_t, dscores)]
    dks = [dot(ds, q) for ds, q in zip(dscores, queries)]
    dvs = [dot(p, g) for p, g in zip(probs, grads)]
    for (rows, index, caps, pair), dq, dk, dv in zip(units, dqs, dks, dvs):
        at = pair * LANES
        back_ref[rows, at : at + LANES] = (fold_heads(dq) * 0.125).astype(BF)
        back_ref[rows, width + at : width + at + LANES] = dk[:SPAN].astype(BF)
        back_ref[rows, 2 * width + at : 2 * width + at + LANES] = dv[:SPAN].astype(BF)
    for pair in range(pairs):
        at = pair * LANES
        dsumm_ref[:, at : at + LANES] += sum(dk[SPAN:] for dk in dks[pair::pairs])
        dsumm_ref[:, width + at : width + at + LANES] += sum(dv[SPAN:] for dv in dvs[pair::pairs])


def with_extra(back, extra, length, begin):
    extra = extra * span_scale(length, begin, extra.shape)
    pos = lax.broadcasted_iota(jnp.int32, back.shape, 0)
    return (back.astype(F32) + jnp.where(pos < length - begin, extra, 0.0)).astype(BF)


GELU_A = 0.7978845608
GELU_B = 0.044715


def gelu_parts(t):
    slow = GELU_A + (GELU_A * GELU_B) * (t * t)
    half = 0.5 * jnp.tanh(t * slow) + 0.5
    value = t * half
    return value, half + (value - value * half) * (6.0 * slow - 4.0 * GELU_A)


MESH = pl.DeviceIdType.MESH


class Place:
    def __init__(self, groups, seqs):
        self.groups, self.seqs, self.chips = groups, seqs, seqs // 2
        self.b = lax.axis_index("batch")
        self.seq = lax.axis_index("seq")
        self.z, self.c = self.seq // 2, self.seq % 2
        self.other = 1 - self.c
        self.b1 = self.b + 1 - 2 * (self.b % 2)
        self.b2 = (self.b + 2) % 4
        self.b3 = self.b1 + 2 - 4 * (self.b1 // 2)
        self.after = [(self.z + k) % self.chips for k in range(self.chips)]
        self.before = [(self.z + self.chips - k) % self.chips for k in range(self.chips)]
        self.sibling = (self.b, 2 * self.z + self.other)
        self.x, self.y, self.diagonal = (self.b1, self.seq), (self.b2, self.seq), (self.b3, self.seq)
        self.along = [(self.b, 2 * z + self.c) for z in self.after]
        self.ring = [(self.b, (self.seq + k) % seqs) for k in range(seqs)]


def meet(place):
    barrier = pltpu.get_barrier_semaphore()
    partners = [place.x, place.y, place.diagonal, *place.ring[1:]]
    for partner in partners:
        pl.semaphore_signal(barrier, inc=1, device_id=partner, device_id_type=MESH)
    pl.semaphore_wait(barrier, len(partners))


def part_of(ref, index):
    return ref if index is None else ref.at[index]


class Copy:
    def __init__(self, make):
        self.make = make
        make().start()

    def wait(self):
        self.make().wait()

    def wait_recv(self):
        self.make().wait_recv()

    def wait_send(self):
        self.make().wait_send()


class Copies:
    def __init__(self, send_sems, recv_sems):
        self.send, self.recv, self.made = send_sems, recv_sems, []

    def start(self, src, src_index, dst, dst_index, device):
        at = len(self.made)
        assert at < self.send.shape[0]
        copy = Copy(
            lambda: pltpu.make_async_remote_copy(
                src_ref=part_of(src, src_index), dst_ref=part_of(dst, dst_index),
                send_sem=self.send.at[at], recv_sem=self.recv.at[at],
                device_id=device, device_id_type=MESH,
            )
        )
        self.made.append(copy)
        return copy

    def push(self, ref, index, device):
        return self.start(ref, index, ref, index, device)

    def finish(self):
        for copy in self.made:
            copy.wait_send()


class Loads:
    def __init__(self, sems):
        self.sems, self.made = sems, 0

    def start(self, src, dst, src_index=None, dst_index=None):
        at = self.made
        assert at < self.sems.shape[0]
        self.made += 1
        return Copy(
            lambda: pltpu.make_async_copy(part_of(src, src_index), part_of(dst, dst_index), self.sems.at[at])
        )


def gather_steps(place, copies, full, rows=slice(None), cols=slice(None)):
    p, half = place, place.chips // 2
    low, high = slice(0, half), slice(half, place.chips)

    def push(b, z, device):
        return copies.push(full, (b, z, p.c, rows, cols), device)

    along = [push(p.b, p.z, device) for device in p.along[1:]]
    yield
    for copy in along:
        copy.wait_recv()
    every = slice(None)
    to_x, to_y, sib = push(p.b, every, p.x), push(p.b, every, p.y), [push(p.b, every, p.sibling)]
    yield
    to_x.wait_recv()
    on_y = push(p.b1, low, p.y)
    to_y.wait_recv()
    on_x = push(p.b2, high, p.x)
    sib += [push(p.b1, every, p.sibling), push(p.b2, every, p.sibling)]
    yield
    on_y.wait_recv()
    sib.append(push(p.b3, low, p.sibling))
    on_x.wait_recv()
    sib.append(push(p.b3, high, p.sibling))
    yield
    for copy in sib:
        copy.wait_recv()


GATHER_COPIES = 12


def fast_gather_steps(place, copies, full, rows=slice(None), cols=slice(None)):
    p = place
    order = range(p.chips)
    early, late = order[: p.chips // 2], order[p.chips // 2 :]

    def push(b, k, device):
        return copies.push(full, (b, p.before[k], p.c, rows, cols), device)

    along = [push(p.b, 0, device) for device in p.along[1:]]
    to_x, to_y, sib = [push(p.b, 0, p.x)], [push(p.b, 0, p.y)], [push(p.b, 0, p.sibling)]
    yield
    for k, copy in enumerate(along, 1):
        copy.wait_recv()
        to_x.append(push(p.b, k, p.x))
        to_y.append(push(p.b, k, p.y))
        sib.append(push(p.b, k, p.sibling))
    yield
    on = []
    for k in early:
        to_x[k].wait_recv()
        on.append(push(p.b1, k, p.y))
        sib.append(push(p.b1, k, p.sibling))
    for k in late:
        to_y[k].wait_recv()
        on.append(push(p.b2, k, p.x))
        sib.append(push(p.b2, k, p.sibling))
    yield
    for k in late:
        to_x[k].wait_recv()
        sib.append(push(p.b1, k, p.sibling))
    for k in early:
        to_y[k].wait_recv()
        sib.append(push(p.b2, k, p.sibling))
    for k, copy in enumerate(on):
        copy.wait_recv()
        sib.append(push(p.b3, k, p.sibling))
    yield
    for copy in sib:
        copy.wait_recv()


def fast_gather_copies(chips):
    return chips - 1 + 3 * chips + 4 * chips


def scatter_steps(place, copies, loads, grad, acc, got, near, far, last, result):
    p, half = place, place.chips // 2
    low, high = slice(0, half), slice(half, place.chips)
    chips = p.chips

    def add(into, *others):
        total = acc[into].astype(F32)
        for other in others:
            total = total + other.astype(F32)
        acc[into] = total.astype(BF)

    every = slice(None)
    swap = copies.start(grad, (every, every, p.other), got, None, p.sibling)
    keep = loads.start(grad, acc, (every, every, p.c))
    yield
    keep.wait()
    swap.wait_recv()
    for b in (p.b3, p.b1, p.b2):
        for z in range(chips):
            add((b, z), got[b, z])
    on_y = copies.start(acc, (p.b3, low), far, 0, p.y)
    on_x = copies.start(acc, (p.b3, high), far, 1, p.x)
    early_x = copies.start(acc, (p.b1, high), near, (0, high), p.x)
    early_y = copies.start(acc, (p.b2, low), near, (1, low), p.y)
    for z in range(chips):
        add((p.b, z), got[p.b, z])
    yield
    on_y.wait_recv()
    for z in range(half):
        add((p.b1, z), far[0, z])
    late_x = copies.start(acc, (p.b1, low), near, (0, low), p.x)
    on_x.wait_recv()
    for z in range(half, chips):
        add((p.b2, z), far[1, z - half])
    late_y = copies.start(acc, (p.b2, high), near, (1, high), p.y)
    yield
    for copy in (early_x, early_y, late_x, late_y):
        copy.wait_recv()
    for z in range(chips):
        add((p.b, z), near[0, z], near[1, z])
    along = []
    for k in range(1, chips):
        along.append(copies.start(acc, (p.b, p.after[k]), last, k - 1, p.along[k]))
    yield
    total = acc[p.b, p.z].astype(F32)
    for k, copy in enumerate(along):
        copy.wait_recv()
        total = total + last[k].astype(F32)
    result[...] = total


SCATTER_COPIES = 10


def scatter_scratch(groups, chips, rows, cols):
    half = chips // 2
    return [
        pltpu.VMEM((groups, chips, rows, cols), BF),
        pltpu.VMEM((groups, chips, rows, cols), BF),
        pltpu.VMEM((2, chips, rows, cols), BF),
        pltpu.VMEM((2, half, rows, cols), BF),
        pltpu.VMEM((chips - 1, rows, cols), BF),
    ]


def share_sum_steps(place, copies, mine, along, across, result):
    p, seqs = place, along.shape[0]
    along[p.seq] = mine[...]
    sent = [copies.push(along, p.seq, device) for device in p.ring[1:]]
    yield
    for copy in sent:
        copy.wait_recv()
    across[p.b] = sum(along[s] for s in range(seqs))
    sent = [copies.push(across, p.b, device) for device in (p.x, p.y, p.diagonal)]
    yield
    for copy in sent:
        copy.wait_recv()
    result[...] = sum(across[b] for b in range(p.groups))


def share_copies(groups, seqs):
    return groups + seqs - 2


class Ticker:
    def __init__(self, *starts):
        self.waiting, self.time = list(starts), 0

    def __call__(self):
        for start, steps in reversed(self.waiting):
            if self.time >= start:
                next(steps, None)
        self.time += 1

    def finish(self):
        run_all(*(steps for _, steps in self.waiting))


def tick(*steps):
    for step in steps:
        next(step, None)


def run_all(*steps):
    live = list(steps)
    while live:
        for step in list(live):
            try:
                next(step)
            except StopIteration:
                live.remove(step)


def loop(count, body, ticks=None):
    def step(index, carry):
        body(index)
        for k in sorted(ticks or {}):
            pl.when(index == k)(lambda run=ticks[k]: run())
        return carry

    lax.fori_loop(0, count, step, 0)


def adam(grad, master, first, second, rate, moment_out, square_out, fresh_out):
    fix = 1.0 - BETA**STEP
    moment = BETA * first + (1.0 - BETA) * grad
    square = BETA * second + (1.0 - BETA) * grad * grad
    update = moment / fix / (jnp.sqrt(square / fix) + ADAM_EPS)
    moment_out[...] = moment
    square_out[...] = square
    fresh_out[...] = master - rate * (update + DECAY * master)


def update_kernel(
    parts, total_ref, qkv_grad, pu_grad, down_grad, norm_grad, outputs_hbm, input_grad_hbm, *refs
):
    state, outs, (outputs_ref, input_ref, sems) = refs[:15], refs[15:-3], refs[-3:]
    outputs_out, input_out, norm_out, moments, squares, fresh = outs[0], outs[1], outs[2], outs[3:8], outs[8:13], outs[13:18]
    loads = Loads(sems)
    ways = ((input_grad_hbm, input_ref, input_out), (outputs_hbm, outputs_ref, outputs_out))
    reads = [Sliced(loads, src, via, parts).start_all() for src, via, _ in ways]
    stores = [Sliced(loads, via, dst, parts) for _, via, dst in ways]
    grad_norm = jnp.sqrt(total_ref[0:1, 0:1])
    norm_out[...] = grad_norm
    factor = jnp.minimum(1.0, CLIP / (grad_norm + 1e-06))
    width = state[1].shape[1]
    piece = state[4].shape[1]
    per = LANES // piece
    index = lax.axis_index("batch") * lax.axis_size("seq") + lax.axis_index("seq")
    block = norm_grad[:, pl.ds(pl.multiple_of(index // per * LANES, LANES), LANES)]
    own = pltpu.roll(block, (LANES - index % per * piece) % LANES, 1)[:, :piece]
    grads = (qkv_grad[...], pu_grad[:, :width], pu_grad[:, width:], down_grad[...], own)
    for at, (grad, rate) in enumerate(zip(grads, RATES)):
        adam(
            grad * factor, state[at][...], state[5 + at][...], state[10 + at][...], rate,
            moments[at], squares[at], fresh[at],
        )
    outs[18][...] = own[3:4] * factor
    for read, store in zip(reads, stores):
        for part in range(parts):
            read.wait(part)
            store.start(part)
    for store in stores:
        store.wait_all()


def cast_shards(p, seqs, qkv_ref, proj_ref, up_ref, down_ref, norm_ref, qkv_full, pu_full, down_full, norm_full):
    width = proj_ref.shape[1]
    b, z, c = p.b, p.z, p.c
    index = b * seqs + 2 * z + c
    qkv_full[b, z, c] = qkv_ref[...].astype(BF)
    pu_full[b, z, c, :, :width] = proj_ref[...].astype(BF)
    pu_full[b, z, c, :, width:] = up_ref[...].astype(BF)
    down_full[b, z, c] = down_ref[...].astype(BF)
    piece = norm_ref.shape[1]
    per = LANES // piece
    tiled = jnp.concatenate([norm_ref[...].astype(BF).astype(F32)] * per, axis=1)
    lane = lax.broadcasted_iota(jnp.int32, tiled.shape, 1)
    norm_full[b, z, c] = jnp.where(lane // piece == index % per, tiled, 0.0)


def join_norms(norm_full, seqs, per, norms_out):
    for block in range(norms_out.shape[1] // LANES):
        total = None
        for device in range(block * per, (block + 1) * per):
            one = norm_full[device // seqs, device % seqs // 2, device % 2]
            total = one if total is None else total + one
        norms_out[:, block * LANES : (block + 1) * LANES] = total


class Sliced:
    def __init__(self, loads, src, dst, count):
        self.src, self.dst, self.count, self.size = src, dst, count, src.shape[0] // count
        self.sems, self.first = loads.sems, loads.made
        loads.made += count
        assert loads.made <= loads.sems.shape[0]

    def copy(self, index):
        begin = index * self.size
        here = pl.ds(begin if isinstance(index, int) else pl.multiple_of(begin, self.size), self.size)
        return pltpu.make_async_copy(self.src.at[here], self.dst.at[here], self.sems.at[self.first + index])

    def start(self, index):
        self.copy(index).start()

    def wait(self, index):
        self.copy(index).wait()

    def start_next(self, index):
        pl.when(index < self.count)(lambda: self.start(index))

    def start_all(self):
        for index in range(self.count):
            self.start(index)
        return self

    def wait_all(self):
        for index in range(self.count):
            self.wait(index)


class SummaryView:
    def __init__(self, ref, rows):
        self.ref, self.rows = ref, rows

    def __getitem__(self, key):
        cols = key[1]
        return self.ref[:, :, :, cols].reshape(self.rows, cols.stop - cols.start)


def row_block(index, size):
    return pl.ds(pl.multiple_of(index * size, size), size)


TILE = 512


def front_kernel(
    groups, seqs, length_ref, x_hbm, og_hbm, qkv_ref, proj_ref, up_ref, down_ref, norm_ref,
    qkv_hbm, pu_hbm, down_hbm, norms_out, mixed_hbm, summ_ref, attn_hbm, lse_ref,
    outputs_hbm, resid_hbm, slope_hbm, down_grad_hbm,
    x_ref, og_ref, qkv_full, pu_full, down_full, mixed_ref, attn_ref, outputs_ref, resid_ref, activ_ref, slope_ref,
    down_grad_ref, norm_full, sum_scr, vt_scr, load_sems, send_sems, recv_sems,
):
    p = Place(groups, seqs)
    rows, width = x_ref.shape
    hidden = activ_ref.shape[1]
    local = rows // SPAN
    length, first_span = length_ref[0], p.seq * local
    count, per = rows // TILE, TILE // SPAN
    loads = Loads(load_sems)
    x_load = Sliced(loads, x_hbm, x_ref, count).start_all()
    cast_shards(
        p, seqs, qkv_ref, proj_ref, up_ref, down_ref, norm_ref, qkv_full, pu_full, down_full, norm_full
    )
    meet(p)
    og_load = loads.start(og_hbm, og_ref)
    copies = Copies(send_sems, recv_sems)
    half_down, half_pu = down_full.shape[3] // 2, pu_full.shape[4] // 2
    in_kv = fast_gather_steps(p, copies, qkv_full, cols=slice(width, 3 * width))
    in_norm = gather_steps(p, copies, norm_full)
    ticker = Ticker(
        (0, gather_steps(p, copies, qkv_full, cols=slice(0, width))),
        (1, gather_steps(p, copies, pu_full, cols=slice(0, half_pu))),
        (2, gather_steps(p, copies, pu_full, cols=slice(half_pu, 2 * half_pu))),
        (3, gather_steps(p, copies, down_full, rows=slice(0, half_down))),
        (4, gather_steps(p, copies, down_full, rows=slice(half_down, 2 * half_down))),
    )
    xhat_ref = resid_ref

    def center(index):
        here = row_block(index, TILE)
        x_load.wait(index)
        xhat_ref[here, :] = normalize(x_ref[here, :].astype(F32))[0]

    tick(in_norm, in_kv)

    def first():
        tick(in_norm, in_kv)
        ticker()

    def second():
        tick(in_norm, in_kv)

    def third():
        tick(in_norm, in_kv)
        ticker()

    loop(count, center, {0: first, count // 2: second, count - 1: third})
    tick(in_norm, in_kv)
    join_norms(norm_full, seqs, LANES // norm_ref.shape[1], norms_out)
    gain, shift = norms_out[0:1, :], norms_out[1:2, :]

    def columns(full, begin, size):
        return full[:, :, :, :, begin : begin + size].reshape(width, size)

    def normed_of(here):
        return (xhat_ref[here, :] * gain + shift).astype(BF)

    def keys_values(index):
        here = row_block(index, TILE)
        mixed = dot(normed_of(here), columns(qkv_full, width, 2 * width)).astype(BF)
        mixed_ref[here, width:] = mixed
        for part in range(per):
            span = index * per + part
            sum_scr[pl.ds(span, 1), :] = span_sum(
                mixed[part * SPAN : (part + 1) * SPAN], length, (first_span + span) * SPAN
            )

    loop(count, keys_values, {0: ticker, count // 2: ticker})
    summ_ref[p.z, p.c] = sum_scr[...].astype(BF)
    along = [copies.push(summ_ref, (p.z, p.c), device) for device in p.along[1:]]
    sib = [copies.push(summ_ref, (p.z, p.c), p.sibling)]
    ticker()
    stores = [loads.start(qkv_full, qkv_hbm)]
    mixed_store = Sliced(loads, mixed_ref, mixed_hbm, count)

    def queries(index):
        here = row_block(index, TILE)
        mixed_ref[here, :width] = dot(normed_of(here), columns(qkv_full, 0, width)).astype(BF)
        mixed_store.start(index)

    loop(count, queries)
    for k, copy in enumerate(along, 1):
        copy.wait_recv()
        sib.append(copies.push(summ_ref, (p.before[k], p.c), p.sibling))
    for copy in sib:
        copy.wait_recv()
    vt_scr[...] = summ_ref[:, :, :, width:].reshape(local * seqs, width).T
    summ_rows = SummaryView(summ_ref, local * seqs)
    attn_store = Sliced(loads, attn_ref, attn_hbm, count)

    def attend(index):
        spans = []
        for k in range(per):
            span = index * per + k
            spans.append((pl.multiple_of(span * SPAN, SPAN), span, span_caps(length, first_span + span)))
        attend_spans(spans, mixed_ref, width, summ_rows, vt_scr, attn_ref, lse_ref)
        attn_store.start(index)

    loop(count, attend, {k: ticker for k in range(1, count, 2)})
    gain_two, shift_two = norms_out[2:3, :], norms_out[3:4, :]
    resid_store, slope_store = (
        Sliced(loads, src, dst, count) for src, dst in ((resid_ref, resid_hbm), (slope_ref, slope_hbm))
    )
    chunk = 256

    def expand(index):
        here = row_block(index, TILE)
        resid = x_ref[here, :].astype(F32) + dot(attn_ref[here, :], columns(pu_full, 0, width))
        resid_ref[here, :] = resid
        resid_store.start(index)
        normed = (normalize(resid)[0] * gain_two + shift_two).astype(BF)
        for at in range(0, hidden, chunk):
            value, slope = gelu_parts(dot(normed, columns(pu_full, width + at, chunk)))
            activ_ref[here, at : at + chunk] = value.astype(BF)
            slope_ref[here, at : at + chunk] = slope.astype(BF)
        slope_store.start(index)

    loop(count, expand, {k: ticker for k in range(1, count, 2)})
    stores.append(loads.start(pu_full, pu_hbm))
    og_load.wait()
    parts = hidden // TILE
    grad_store = Sliced(loads, down_grad_ref, down_grad_hbm, parts)

    def down_grad(index):
        here = row_block(index, TILE)
        down_grad_ref[here, :] = dot_tn(activ_ref[:, here], og_ref[...]).astype(BF)
        grad_store.start(index)

    loop(parts, down_grad)
    ticker.finish()
    stores.append(loads.start(down_full, down_hbm))
    outputs_store = Sliced(loads, outputs_ref, outputs_hbm, count)

    def contract(index):
        here = row_block(index, TILE)
        out = resid_ref[here, :] + dot(activ_ref[here, :], down_full[...].reshape(hidden, width))
        outputs_ref[here, :] = out.astype(BF)
        outputs_store.start(index)

    loop(count, contract)
    for store in (mixed_store, attn_store, resid_store, slope_store, grad_store, outputs_store):
        store.wait_all()
    for store in stores:
        store.wait()
    copies.finish()


def middle_kernel(
    groups, seqs, og_hbm, resid_hbm, slope_hbm, attn_hbm, pu_hbm, down_hbm, norms_ref, down_grad_hbm,
    resid_grad_hbm, attn_grad_hbm, pu_grad_hbm, down_out, norm_grad_ref,
    og_ref, resid_ref, slope_ref, attn_ref, pu_ref, down_ref, resid_grad_ref, attn_grad_ref, pu_grad_ref,
    pre_grad_ref, normed_ref, pig_ref, *scratch,
):
    *buffers, load_sems, send_sems, recv_sems = scratch
    p = Place(groups, seqs)
    rows, width = og_ref.shape
    hidden = slope_ref.shape[1]
    count = rows // TILE
    loads = Loads(load_sems)
    early = [loads.start(down_hbm, down_ref)]
    tiled = [
        Sliced(loads, src, dst, count)
        for src, dst in ((og_hbm, og_ref), (slope_hbm, slope_ref), (resid_hbm, resid_ref))
    ]
    for load in tiled:
        load.start(0)
    early.append(loads.start(pu_hbm, pu_ref))
    for load in tiled:
        load.start(1)
    meet(p)
    copies = Copies(send_sems, recv_sems)
    half = down_out.shape[0] // 2
    ticker = Ticker(
        *(
            (
                at,
                scatter_steps(
                    p, copies, loads, down_grad_hbm.at[:, :, :, half * at : half * (at + 1)], *buffers[5 * at : 5 * at + 5],
                    down_out.at[half * at : half * (at + 1)],
                ),
            )
            for at in range(2)
        )
    )
    ticker()
    attn_load = loads.start(attn_hbm, attn_ref)
    norm_grad_ref[...] = jnp.zeros_like(norm_grad_ref)
    resid_grad_store, attn_grad_store = (
        Sliced(loads, src, dst, count)
        for src, dst in ((resid_grad_ref, resid_grad_hbm), (attn_grad_ref, attn_grad_hbm))
    )
    gain, shift = norms_ref[2:3, :], norms_ref[3:4, :]
    chunk = 256
    early[0].wait()

    def tile(index):
        here = row_block(index, TILE)
        for load in tiled:
            load.start_next(index + 2)
            load.wait(index)
        grad = og_ref[here, :]
        for at in range(0, hidden, chunk):
            act_grad = dot_nt(grad, down_ref[at : at + chunk, :])
            slope = slope_ref[here, at : at + chunk].astype(F32)
            pre_grad_ref[here, at : at + chunk] = (act_grad * slope).astype(BF)

        @pl.when(index == 0)
        def _():
            early[1].wait()

        back = dot_nt(pre_grad_ref[here, :], pu_ref[:, width:])
        xhat, rstd = normalize(resid_ref[here, :])
        normed_ref[here, :] = (xhat * gain + shift).astype(BF)
        resid_grad = grad.astype(F32) + norm_back(back, gain, xhat, rstd)
        resid_grad_ref[here, :] = resid_grad
        resid_grad_store.start(index)
        pig = resid_grad.astype(BF)
        pig_ref[here, :] = pig
        attn_grad_ref[here, :] = dot_nt(pig, pu_ref[:, :width]).astype(BF)
        attn_grad_store.start(index)
        norm_grad_ref[0:1, :] += jnp.sum(back * xhat, axis=0, keepdims=True)
        norm_grad_ref[1:2, :] += jnp.sum(back, axis=0, keepdims=True)

    loop(count, tile, {k: ticker for k in range(count)})
    attn_load.wait()
    pu_grad_ref[:, :width] = dot_tn(attn_ref[...], pig_ref[...]).astype(BF)

    def up_grad(index):
        at = pl.multiple_of(width + index * TILE, TILE)
        pu_grad_ref[:, pl.ds(at, TILE)] = dot_tn(normed_ref[...], pre_grad_ref[:, row_block(index, TILE)]).astype(BF)

    loop(hidden // TILE, up_grad, {1: ticker})
    pu_store = loads.start(pu_grad_ref, pu_grad_hbm)
    resid_grad_store.wait_all()
    attn_grad_store.wait_all()
    ticker.finish()
    pu_store.wait()
    copies.finish()


def back_kernel(
    groups, seqs, length_ref, x_hbm, mixed_hbm, grad_hbm, lse_ref, summ_ref, pu_hbm, resid_grad_hbm, down_ref,
    norms_ref, weight_hbm, norm_two_ref,
    input_grad_hbm, qkv_out, pu_out, norm_out, total_out,
    x_ref, mixed_ref, grad_ref, resid_grad_ref, weight_ref, input_grad_ref,
    mg_scr, xhat_ref, kt_scr, dsumm_scr, dsumm_got, dsumm_low, dsumm_last, extra_scr, q_grad, k_grad, v_grad,
    gain_cols, shift_cols,
    *scratch,
):
    *buffers, norm_mine, along_norm, across_norm, sq_mine, along_sq, across_sq = scratch[:-3]
    load_sems, send_sems, recv_sems = scratch[-3:]
    p = Place(groups, seqs)
    rows, width = x_ref.shape
    local = rows // SPAN
    length, first_span = length_ref[0], p.seq * local
    loads = Loads(load_sems)
    group = 2
    count, steps = rows // TILE, local // group
    reads = [
        Sliced(loads, src, dst, steps) for src, dst in ((mixed_hbm, mixed_ref), (grad_hbm, grad_ref))
    ]
    for index in range(2):
        for read in reads:
            read.start(index)
    meet(p)
    copies = Copies(send_sems, recv_sems)

    def scatter(grad, at, out):
        return scatter_steps(p, copies, loads, grad, *buffers[5 * at : 5 * at + 5], out)

    half = pu_hbm.shape[4] // 2
    ticker = Ticker(
        *((at, scatter(pu_hbm.at[:, :, :, :, half * at : half * (at + 1)], at, pu_out.at[:, half * at : half * (at + 1)]))
          for at in range(2))
    )
    ticker()
    late = [loads.start(src, dst) for src, dst in ((x_hbm, x_ref), (weight_hbm, weight_ref))]
    resid_grad_load = loads.start(resid_grad_hbm, resid_grad_ref)
    kt_scr[...] = summ_ref[:, :width].T
    dsumm_scr[...] = jnp.zeros_like(dsumm_scr)

    def attend_back(index):
        for read in reads:
            read.start_next(index + 2)
            read.wait(index)
        each = []
        for k in range(group):
            span = index * group + k
            each.append((pl.multiple_of(span * SPAN, SPAN), span, span_caps(length, first_span + span)))
        attend_back_spans(each, mixed_ref, grad_ref, width, summ_ref, kt_scr, lse_ref, mg_scr, dsumm_scr)

    loop(steps, attend_back, {at: ticker for at in range(0, steps, 2)})
    swap = []
    for z in range(p.chips):
        block = pl.ds(pl.multiple_of((2 * z + p.other) * local, local), local)
        swap.append(copies.start(dsumm_scr, block, dsumm_got, z, p.sibling))
    gain, shift = norms_ref[0:1, :], norms_ref[1:2, :]
    for read in late:
        read.wait()

    def recompute(index):
        here = row_block(index, TILE)
        xhat_ref[here, :] = normalize(x_ref[here, :].astype(F32))[0].astype(BF)

    loop(count // 2, recompute)
    for copy in swap:
        copy.wait_recv()

    def half_sum(z):
        mine = dsumm_scr[pl.ds(pl.multiple_of((2 * z + p.c) * local, local), local), :]
        return mine + dsumm_got[z]

    along = []
    for k in range(1, p.chips):
        dsumm_low[k - 1] = half_sum(p.after[k]).astype(BF)
        along.append(copies.start(dsumm_low, k - 1, dsumm_last, k - 1, p.along[k]))
    loop(count // 2, lambda index: recompute(index + count // 2))
    per_block = width // (groups * seqs)
    gain_cols[...] = jnp.broadcast_to(gain, (LANES, width)).T
    shift_cols[...] = jnp.broadcast_to(shift, (LANES, width)).T

    def weight_grad(into, at):
        begin = at * width
        back = mg_scr[:, begin : begin + width]
        moved = dot_tn(xhat_ref[...], back)
        total = jnp.sum(back.astype(F32), axis=0, keepdims=True)
        blocks, gains, shifts = [], 0.0, 0.0
        for k in range(0, width, LANES):
            part, sums = moved[:, k : k + LANES], total[:, k : k + LANES]
            blocks.append(gain_cols[...] * part + shift_cols[...] * sums)
            weight = weight_ref[:, begin + k : begin + k + LANES].astype(F32)
            gains += weight * part
            shifts += weight * sums
        into[...] = jnp.concatenate(blocks, axis=1).astype(BF).reshape(groups, p.chips, 2, per_block, width)
        gain_sums = jnp.sum(gains.T, axis=0, keepdims=True)
        shift_sums = jnp.sum(shifts.T, axis=0, keepdims=True)
        norm_mine[0:1, :] = gain_sums + (norm_mine[0:1, :] if at else 0.0)
        norm_mine[1:2, :] = shift_sums + (norm_mine[1:2, :] if at else 0.0)

    norm_mine[2:4, :] = norm_two_ref[...]
    outs = [qkv_out.at[:, width * at : width * (at + 1)] for at in range(3)]
    weight_grad(q_grad, 0)
    out_q = scatter(q_grad, 2, outs[0])
    tick(out_q)
    ticker()

    def back_q(index):
        here = row_block(index, TILE)
        input_grad_ref[here, :] = dot_nt(mg_scr[here, :width], weight_ref[:, :width])

    loop(count, back_q)
    tick(out_q)
    ticker()
    total = half_sum(p.z)
    for k, copy in enumerate(along):
        copy.wait_recv()
        total = total + dsumm_last[k].astype(F32)
    extra_scr[...] = total

    def add_extra(index):
        for k in range(2):
            span = index * 2 + k
            here = row_block(span, SPAN)
            mg_scr[here, width:] = with_extra(
                mg_scr[here, width:], extra_scr[pl.ds(span, 1), :], length, (first_span + span) * SPAN
            )

    loop(local // 2, add_extra)
    weight_grad(k_grad, 1)
    out_k = scatter(k_grad, 3, outs[1])
    tick(out_k, out_q)
    weight_grad(v_grad, 2)
    out_v = scatter(v_grad, 4, outs[2])
    norm_sum = share_sum_steps(p, copies, norm_mine, along_norm, across_norm, norm_out)
    tick(out_v, norm_sum, out_k, out_q)
    ticker()
    resid_grad_load.wait()
    store = Sliced(loads, input_grad_ref, input_grad_hbm, count)

    def finish(index):
        here = row_block(index, TILE)
        xhat, rstd = normalize(x_ref[here, :].astype(F32))
        back = input_grad_ref[here, :] + dot_nt(mg_scr[here, width:], weight_ref[:, width:])
        input_grad_ref[here, :] = resid_grad_ref[here, :] + norm_back(back, gain, xhat, rstd)
        store.start(index)

    def advance():
        tick(out_v, norm_sum, out_k, out_q)
        ticker()

    loop(count, finish, {k: advance for k in range(0, count, 2)})
    run_all(out_v, norm_sum, out_k, out_q)
    ticker.finish()
    local_sum = sum(jnp.sum(jnp.square(out[...]), keepdims=True) for out in (qkv_out, pu_out, down_ref))
    sq_mine[...] = jnp.broadcast_to(local_sum, sq_mine.shape)
    run_all(share_sum_steps(p, copies, sq_mine, along_sq, across_sq, total_out))
    total_out[...] = total_out[...] + jnp.sum(jnp.square(norm_out[...]), keepdims=True)
    store.wait_all()
    copies.finish()


def qkv_kernel(info_ref, x_ref, norms_ref, weight_ref, mixed_ref, summ_ref, sum_scr):
    step = pl.program_id(0)
    tile, width = x_ref.shape
    length, first_span = info_ref[0], info_ref[1]
    mixed = qkv_tile(x_ref[...], norms_ref, weight_ref)
    mixed_ref[...] = mixed
    per = tile // SPAN
    for part in range(per):
        span = step * per + part
        sum_scr[pl.ds(span, 1), :] = span_sum(
            mixed[part * SPAN : (part + 1) * SPAN, width:], length, (first_span + span) * SPAN
        )

    @pl.when(step == pl.num_programs(0) - 1)
    def _():
        summ_ref[...] = sum_scr[...].astype(BF)


def attend_kernel(info_ref, mixed_ref, summ_ref, out_ref, lse_ref, vt_scr):
    step = pl.program_id(0)
    width = out_ref.shape[1]

    @pl.when(step == 0)
    def _():
        vt_scr[...] = summ_ref[:, width:].T

    caps = span_caps(info_ref[0], info_ref[1] + step)
    attend_spans([(0, 0, caps)], mixed_ref, width, summ_ref, vt_scr, out_ref, lse_ref)


def attend_back_kernel(info_ref, mixed_ref, grad_ref, lse_ref, summ_ref, back_ref, dsumm_ref, kt_scr):
    step = pl.program_id(0)
    width = grad_ref.shape[1]

    @pl.when(step == 0)
    def _():
        kt_scr[...] = summ_ref[:, :width].T
        dsumm_ref[...] = jnp.zeros_like(dsumm_ref)

    caps = span_caps(info_ref[0], info_ref[1] + step)
    attend_back_spans(
        [(0, 0, caps)], mixed_ref, grad_ref, width, summ_ref, kt_scr, lse_ref, back_ref, dsumm_ref
    )


def mlp_kernel(
    x_ref, attn_ref, og_ref, norms_ref, pu_ref, down_ref,
    out_ref, resid_grad_ref, attn_grad_ref, pu_grad_ref, down_grad_ref, norm_grad_ref,
    activ_scr, pre_grad_scr, n2t_scr, attnt_scr, ogt_scr, pig_scr, norm_scr,
):
    step = pl.program_id(0)
    tile, width = x_ref.shape
    hidden = down_ref.shape[0]
    rows = pl.ds(pl.multiple_of(step * tile, tile), tile)
    chunk = 256
    attn = attn_ref[...]
    grad = og_ref[...]
    resid = x_ref[...].astype(F32) + dot(attn, pu_ref[:, :width])
    xhat, rstd = normalize(resid)
    gain = norms_ref[2:3, :]
    normed = (xhat * gain + norms_ref[3:4, :]).astype(BF)
    attnt_scr[:, rows] = attn.T
    n2t_scr[:, rows] = normed.T
    ogt_scr[:, rows] = grad.T
    for at in range(0, hidden, chunk):
        pre = dot(normed, pu_ref[:, width + at : width + at + chunk])
        act_grad = dot_nt(grad, down_ref[at : at + chunk, :])
        value, slope = gelu_parts(pre)
        activ = value.astype(BF)
        pre_grad = (act_grad * slope).astype(BF)
        activ_scr[rows, at : at + chunk] = activ
        pre_grad_scr[rows, at : at + chunk] = pre_grad
    out_ref[...] = (resid + dot(activ_scr[rows, :], down_ref[...])).astype(BF)
    back = dot_nt(pre_grad_scr[rows, :], pu_ref[:, width:])
    resid_grad = grad.astype(F32) + norm_back(back, gain, xhat, rstd)
    resid_grad_ref[...] = resid_grad
    pig = resid_grad.astype(BF)
    pig_scr[rows, :] = pig
    attn_grad_ref[...] = dot_nt(pig, pu_ref[:, :width]).astype(BF)
    gain_part = jnp.sum(back * xhat, axis=0, keepdims=True)
    shift_part = jnp.sum(back, axis=0, keepdims=True)
    part = jnp.concatenate([gain_part, shift_part], axis=0)

    @pl.when(step == 0)
    def _():
        norm_scr[...] = part

    @pl.when(step > 0)
    def _():
        norm_scr[...] += part

    @pl.when(step == pl.num_programs(0) - 1)
    def _():
        norm_grad_ref[...] = norm_scr[...]
        pu_grad_ref[:, :width] = dot(attnt_scr[...], pig_scr[...]).astype(BF)
        cols = 512

        def one(index, carry):
            c = pl.ds(pl.multiple_of(index * cols, cols), cols)
            out = pl.ds(pl.multiple_of(width + index * cols, cols), cols)
            pu_grad_ref[:, out] = dot(n2t_scr[...], pre_grad_scr[:, c]).astype(BF)
            down_grad_ref[c, :] = dot(ogt_scr[...], activ_scr[:, c]).T.astype(BF)
            return carry

        lax.fori_loop(0, hidden // cols, one, 0)


def final_kernel(
    info_ref, x_ref, back_ref, extra_ref, resid_grad_ref, norms_ref, weight_ref,
    input_grad_ref, qkv_grad_ref, norm_grad_ref, mg_scr, normed_scr,
):
    step = pl.program_id(0)
    tile, width = x_ref.shape
    rows = pl.ds(pl.multiple_of(step * tile, tile), tile)
    length, first_span = info_ref[0], info_ref[1]
    xhat, rstd = normalize(x_ref[...].astype(F32))
    gain = norms_ref[0:1, :]
    normed_scr[rows, :] = (xhat * gain + norms_ref[1:2, :]).astype(BF)
    per = tile // SPAN
    parts = []
    for part in range(per):
        span = step * per + part
        here = back_ref[part * SPAN : (part + 1) * SPAN, width:]
        parts.append(with_extra(here, extra_ref[pl.ds(span, 1), :], length, (first_span + span) * SPAN))
    mg = jnp.concatenate([back_ref[:, :width], jnp.concatenate(parts, axis=0)], axis=1)
    mg_scr[rows, :] = mg
    back = dot_nt(mg, weight_ref[...])
    input_grad_ref[...] = resid_grad_ref[...] + norm_back(back, gain, xhat, rstd)

    @pl.when(step == 0)
    def _():
        norm_grad_ref[...] = jnp.zeros_like(norm_grad_ref)

    norm_grad_ref[0:1, :] += jnp.sum(back * xhat, axis=0, keepdims=True)
    norm_grad_ref[1:2, :] += jnp.sum(back, axis=0, keepdims=True)

    @pl.when(step == pl.num_programs(0) - 1)
    def _():
        cols = 256

        def one(index, carry):
            c = pl.ds(pl.multiple_of(index * cols, cols), cols)
            qkv_grad_ref[:, c] = dot_tn(normed_scr[...], mg_scr[:, c]).astype(BF)
            return carry

        lax.fori_loop(0, qkv_grad_ref.shape[1] // cols, one, 0)


def whole(shape):
    return pl.BlockSpec(shape, lambda i: (0,) * len(shape))


def by_rows(tile, width):
    return pl.BlockSpec((tile, width), lambda i: (i, 0))


SCALARS = pl.BlockSpec(memory_space=pltpu.SMEM)
PARAMS = pltpu.CompilerParams(vmem_limit_bytes=VMEM_LIMIT)


def remote_call(kernel, groups, seqs, name, collective_id, outs, ins, scratch, loads, copies):
    return pl.pallas_call(
        functools.partial(kernel, groups, seqs),
        in_specs=[pl.BlockSpec(memory_space=space) for space in ins],
        out_specs=[pl.BlockSpec(memory_space=space) for space, _, _ in outs],
        out_shape=[jax.ShapeDtypeStruct(shape, kind) for _, shape, kind in outs],
        scratch_shapes=list(scratch) + [pltpu.SemaphoreType.DMA((n,)) for n in (loads, copies, copies)],
        compiler_params=pltpu.CompilerParams(
            vmem_limit_bytes=VMEM_LIMIT, collective_id=collective_id, has_side_effects=True
        ),
        name=name,
    )


def regroup(grad, dim, outer, inner):
    shape = grad.shape
    piece = shape[dim] // (outer * inner)
    split = grad.reshape(shape[:dim] + (outer, inner, piece) + shape[dim + 1 :])
    return jnp.swapaxes(split, dim, dim + 1).reshape(shape)


def gather_plain(state):
    both = ("batch", "seq")
    qkv, proj, up, down = (lax.all_gather(w.astype(BF), both, axis=0, tiled=True) for w in state[:4])
    norms = lax.all_gather(state[4].astype(BF), both, axis=1, tiled=True).astype(F32)
    return qkv, jnp.concatenate([proj, up], axis=1), down, norms


def reduce_plain(qkv_grad, pu_grad, down_grad, norm_grad):
    groups, seqs = lax.axis_size("batch"), lax.axis_size("seq")
    reduced = []
    for grad, dim in ((qkv_grad, 0), (pu_grad, 0), (down_grad, 0)):
        part = lax.psum_scatter(
            regroup(grad.astype(F32), dim, groups, seqs), "seq", scatter_dimension=dim, tiled=True
        )
        reduced.append(lax.psum_scatter(part, "batch", scatter_dimension=dim, tiled=True))
    norm_total = lax.psum(norm_grad, ("batch", "seq"))
    squares = lax.psum(sum(jnp.sum(grad * grad) for grad in reduced), ("batch", "seq"))
    squares = squares + jnp.sum(norm_total * norm_total)
    return (*reduced, norm_total, jnp.broadcast_to(squares, (8, LANES)))


def mlp_call(x, attn_out, grad_rows, norms, pu_full, down_full):
    sds = jax.ShapeDtypeStruct
    rows, width = x.shape
    hidden = down_full.shape[0]
    tile = min(512, rows)
    steps = rows // tile
    return pl.pallas_call(
        mlp_kernel,
        grid=(steps,),
        in_specs=[by_rows(tile, width)] * 3
        + [whole(norms.shape), whole(pu_full.shape), whole(down_full.shape)],
        out_specs=[by_rows(tile, width)] * 3
        + [whole(pu_full.shape), whole(down_full.shape), whole((2, width))],
        out_shape=[
            sds((rows, width), BF), sds((rows, width), F32), sds((rows, width), BF),
            sds(pu_full.shape, BF), sds(down_full.shape, BF), sds((2, width), F32),
        ],
        scratch_shapes=[
            pltpu.VMEM((rows, hidden), BF), pltpu.VMEM((rows, hidden), BF),
            pltpu.VMEM((width, rows), BF), pltpu.VMEM((width, rows), BF), pltpu.VMEM((width, rows), BF),
            pltpu.VMEM((rows, width), BF), pltpu.VMEM((2, width), F32),
        ],
        compiler_params=PARAMS,
        name="mlp",
    )(x, attn_out, grad_rows, norms, pu_full, down_full)


def direct_body(groups, seqs, inputs, out_grad, lengths, *state):
    rows, width = inputs.shape[1], inputs.shape[2]
    own_rows, down_rows = state[0].shape[0], state[3].shape[0]
    hidden = state[2].shape[1]
    chips = seqs // 2
    grid3 = (groups, chips, 2)
    local = rows // SPAN
    spans = local * seqs
    pairs = width // LANES
    count = rows // TILE
    x, grad_rows = inputs[0], out_grad[0]
    vmem, hbm, smem = pltpu.VMEM, pl.ANY, pltpu.SMEM
    shapes = (
        (*grid3, own_rows, 3 * width), (*grid3, own_rows, width + hidden), (*grid3, down_rows, width),
    )
    tokens = (rows, width)
    (
        qkv_full, pu_full, down_full, norms, mixed, summ, attn_out, lse, outputs, resid, slope, down_grad,
    ) = remote_call(
        front_kernel, groups, seqs, "front", 0,
        [
            *((hbm, shape, BF) for shape in shapes), (vmem, (4, width), F32), (hbm, (rows, 3 * width), BF),
            (vmem, (chips, 2, local, 2 * width), BF), (hbm, tokens, BF), (vmem, (local, pairs, 2 * SPAN), F32),
            (hbm, tokens, BF), (hbm, tokens, F32), (hbm, (rows, hidden), BF), (hbm, (hidden, width), BF),
        ],
        [smem, hbm, hbm] + [vmem] * 5,
        [
            vmem(tokens, BF), vmem(tokens, BF), *(vmem(shape, BF) for shape in shapes),
            vmem((rows, 3 * width), BF), vmem(tokens, BF), vmem(tokens, BF), vmem(tokens, F32),
            vmem((rows, hidden), BF), vmem((rows, hidden), BF), vmem((hidden, width), BF),
            vmem((*grid3, 4, LANES), F32), vmem((local, 2 * width), F32), vmem((width, spans), BF),
        ],
        4 + 6 * count + hidden // TILE, 6 * GATHER_COPIES + fast_gather_copies(chips) + 2 * chips,
    )(lengths, x, grad_rows, *state[:5])
    pu_flat, down_flat = pu_full.reshape(width, width + hidden), down_full.reshape(hidden, width)
    resid_grad, attn_grad, pu_grad, down_own, norm_two = remote_call(
        middle_kernel, groups, seqs, "middle", 1,
        [
            (hbm, tokens, F32), (hbm, tokens, BF), (hbm, pu_flat.shape, BF),
            (vmem, (down_rows, width), F32), (vmem, (2, width), F32),
        ],
        [hbm] * 6 + [vmem, hbm],
        [
            vmem(tokens, BF), vmem(tokens, F32), vmem((rows, hidden), BF), vmem(tokens, BF),
            vmem(pu_flat.shape, BF), vmem(down_flat.shape, BF), vmem(tokens, F32), vmem(tokens, BF),
            vmem(pu_flat.shape, BF), vmem((rows, hidden), BF), vmem(tokens, BF), vmem(tokens, BF),
            *scatter_scratch(groups, chips, down_rows // 2, width) * 2,
        ],
        6 + 5 * count, 2 * SCATTER_COPIES,
    )(grad_rows, resid, slope, attn_out, pu_flat, down_flat, norms, down_grad.reshape(shapes[2]))
    half = (width + hidden) // 2
    blocks = ((own_rows, half),) * 2 + ((own_rows, width),) * 3
    summ_block = (local, 2 * width)
    scratch = [
        vmem(tokens, BF), vmem((rows, 3 * width), BF), vmem(tokens, BF), vmem(tokens, F32),
        vmem((width, 3 * width), BF), vmem(tokens, F32),
        vmem((rows, 3 * width), BF), vmem(tokens, BF), vmem((width, spans), BF), vmem((spans, 2 * width), F32),
        vmem((chips, *summ_block), F32), vmem((chips - 1, *summ_block), BF),
        vmem((chips - 1, *summ_block), BF), vmem(summ_block, F32),
        *[vmem((*grid3, own_rows, width), BF)] * 3, *[vmem((width, LANES), F32)] * 2,
    ]
    scratch += [buffer for block in blocks for buffer in scatter_scratch(groups, chips, *block)]
    scratch += [
        vmem((4, width), F32), vmem((seqs, 4, width), F32), vmem((groups, 4, width), F32),
        vmem((8, LANES), F32), vmem((seqs, 8, LANES), F32), vmem((groups, 8, LANES), F32),
    ]
    input_grad, qkv_own, pu_own, norm_total, total = remote_call(
        back_kernel, groups, seqs, "back", 2,
        [
            (hbm, tokens, F32), (vmem, (own_rows, 3 * width), F32), (vmem, (own_rows, width + hidden), F32),
            (vmem, (4, width), F32), (vmem, (8, LANES), F32),
        ],
        [smem, hbm, hbm, hbm, vmem, vmem, hbm, hbm, vmem, vmem, hbm, vmem],
        scratch, local + 3 + 5 + count,
        5 * SCATTER_COPIES + 2 * share_copies(groups, seqs) + 2 * chips,
    )(
        lengths, x, mixed, attn_grad, lse, summ.reshape(spans, 2 * width), pu_grad.reshape(shapes[1]),
        resid_grad, down_own, norms, qkv_full.reshape(width, 3 * width), norm_two,
    )
    return outputs, input_grad, (qkv_own, pu_own, down_own), norm_total, total


def plain_body(groups, seqs, inputs, out_grad, lengths, *state):
    sds = jax.ShapeDtypeStruct
    rows, width = inputs.shape[1], inputs.shape[2]
    qkv_full, pu_full, down_full, norms = gather_plain(state[:5])
    local = rows // SPAN
    spans = local * seqs
    info = jnp.stack([lengths[0], (lax.axis_index("seq") * local).astype(jnp.int32)])
    x, grad_rows = inputs[0], out_grad[0]
    tile = 256
    steps = rows // tile
    mixed, own_summ = pl.pallas_call(
        qkv_kernel,
        grid=(steps,),
        in_specs=[SCALARS, by_rows(tile, width), whole(norms.shape), whole(qkv_full.shape)],
        out_specs=[by_rows(tile, 3 * width), whole((local, 2 * width))],
        out_shape=[sds((rows, 3 * width), BF), sds((local, 2 * width), BF)],
        scratch_shapes=[pltpu.VMEM((local, 2 * width), F32)],
        compiler_params=PARAMS,
        name="qkv",
    )(info, x, norms, qkv_full)
    summ = lax.all_gather(own_summ, "seq", axis=0, tiled=True)
    pairs = width // LANES
    lse_spec = pl.BlockSpec((1, pairs, 2 * SPAN), lambda i: (i, 0, 0))
    attn_out, lse = pl.pallas_call(
        attend_kernel,
        grid=(local,),
        in_specs=[SCALARS, by_rows(SPAN, 3 * width), whole(summ.shape)],
        out_specs=[by_rows(SPAN, width), lse_spec],
        out_shape=[sds((rows, width), BF), sds((local, pairs, 2 * SPAN), F32)],
        scratch_shapes=[pltpu.VMEM((width, spans), BF)],
        compiler_params=PARAMS,
        name="attend",
    )(info, mixed, summ)
    outputs, resid_grad, attn_grad, pu_grad, down_grad, norm_two = mlp_call(
        x, attn_out, grad_rows, norms, pu_full, down_full
    )
    back, dsumm = pl.pallas_call(
        attend_back_kernel,
        grid=(local,),
        in_specs=[SCALARS, by_rows(SPAN, 3 * width), by_rows(SPAN, width), lse_spec, whole(summ.shape)],
        out_specs=[by_rows(SPAN, 3 * width), whole((spans, 2 * width))],
        out_shape=[sds((rows, 3 * width), BF), sds((spans, 2 * width), F32)],
        scratch_shapes=[pltpu.VMEM((width, spans), BF)],
        compiler_params=PARAMS,
        name="attend_back",
    )(info, mixed, attn_grad, lse, summ)
    extra = lax.psum_scatter(dsumm, "seq", scatter_dimension=0, tiled=True)
    input_grad, qkv_grad, norm_one = pl.pallas_call(
        final_kernel,
        grid=(steps,),
        in_specs=[
            SCALARS, by_rows(tile, width), by_rows(tile, 3 * width), whole(extra.shape), by_rows(tile, width),
            whole(norms.shape), whole(qkv_full.shape),
        ],
        out_specs=[by_rows(tile, width), whole(qkv_full.shape), whole((2, width))],
        out_shape=[sds((rows, width), F32), sds(qkv_full.shape, BF), sds((2, width), F32)],
        scratch_shapes=[pltpu.VMEM((rows, 3 * width), BF), pltpu.VMEM((rows, width), BF)],
        compiler_params=PARAMS,
        name="final",
    )(info, x, back, extra, resid_grad, norms, qkv_full)
    norm_grad = jnp.concatenate([norm_one, norm_two], axis=0)
    *grads, norm_total, total = reduce_plain(qkv_grad, pu_grad, down_grad, norm_grad)
    return outputs, input_grad, grads, norm_total, total


def body(groups, seqs, *args):
    state = args[3:]
    direct = groups == 4 and seqs % 4 == 0 and state[0].shape[0] % 16 == 0 and args[0].shape[1] % TILE == 0
    run = direct_body if direct else plain_body
    outputs, input_grad, grads, norm_total, total = run(groups, seqs, *args)
    sds = jax.ShapeDtypeStruct
    vmem, hbm = pltpu.VMEM, pl.ANY
    spec = lambda space: pl.BlockSpec(memory_space=space)
    held = [sds(w.shape, F32) for w in state[:5]]
    parts = 8
    outputs, input_grad, grad_norm, *fresh, shift_clipped = pl.pallas_call(
        functools.partial(update_kernel, parts),
        in_specs=[spec(vmem)] * 5 + [spec(hbm)] * 2 + [spec(vmem)] * 15,
        out_specs=[spec(hbm)] * 2 + [spec(vmem)] * 17,
        out_shape=[
            sds(outputs.shape, BF), sds(input_grad.shape, F32), sds((1, 1), F32), *held * 3,
            sds((1, state[4].shape[1]), F32),
        ],
        scratch_shapes=[
            vmem(outputs.shape, BF), vmem(input_grad.shape, F32), pltpu.SemaphoreType.DMA((4 * parts,)),
        ],
        compiler_params=PARAMS,
        name="update",
    )(total, *grads, norm_total, outputs, input_grad, *state)
    return (outputs[None], input_grad[None], grad_norm[0, 0], *fresh, shift_clipped[0])


def solution(mesh):
    tokens = P("batch", "seq", None)
    owned = P(("batch", "seq"), None)
    columns = P(None, ("batch", "seq"))
    state = (owned, owned, owned, owned, columns)
    return jax.shard_map(
        functools.partial(body, mesh.shape["batch"], mesh.shape["seq"]),
        mesh=mesh,
        in_specs=(tokens, tokens, P("batch")) + state * 3,
        out_specs=(tokens, tokens, P()) + state * 3 + (P(("batch", "seq")),),
        check_vma=False,
    )
```

profile of v0, /device:TPU:0, one launch (start us, length us, event | category | flops | bytes accessed | tf_op | source)
XLA Modules:
  0.0 172.5 jit_solution(13529857965178168563)
XLA Ops:
  1.3 72.8 %front.1 = (bf16[4,4,2,16,1536]{4,3,2,1,0:T(8,128)(2,1)}, bf16[4,4,2,16,2560]{4,3,2,1,0:T(8,128)(2,1)}, bf16[4,4,2,64,512]{4,3,2,1,0:T(8,128)(2,1)}, f32[4,512]{...) custom-call(s32[1]{0:T(128)S(6)} %copy.37.length_ref, ...), custom_call_target="tpu_custom_call" | custom-call | tf_op jit(solution)/shard_map/front/pallas_call | solution.py:1231
  74.1 30.7 %middle.1 = (f32[2048,512]{1,0:T(8,128)}, bf16[2048,512]{1,0:T(8,128)(2,1)}, bf16[512,2560]{1,0:T(8,128)(2,1)}, f32[64,512]{1,0:T(8,128)}, f32[2,512]{1,0:T(2,128)}) custom-call(bf16[2048,512]{1,0:T(8,128)(2,1)} %bitcast.15, f32[2048,512]{1,0:T(8,128)} %get-tuple-element.61.resid_hbm, bf16[2048,2048]{1,0:T(8,128)(2,1)} %get-tuple-element.62.slope_hbm, ...), custom_call_target="tpu_custom_call" | custom-call | tf_op jit(solution)/shard_map/middle/pallas_call | solution.py:1248
  104.8 59.4 %back.1 = (f32[2048,512]{1,0:T(8,128)}, f32[16,1536]{1,0:T(8,128)}, f32[16,2560]{1,0:T(8,128)}, f32[4,512]{1,0:T(4,128)}, f32[8,128]{1,0:T(8,128)}) custom-call(s32[1]{0:T(128)S(6)} %copy.37.length_ref, bf16[2048,512]{1,0:T(8,128)(2,1)} %bitcast.13, bf16[2048,1536]{1,0:T(8,128)(2,1)} %get-tuple-element.60.mixed_hbm, ...), custom_call_target="tpu_custom_call" | custom-call | tf_op jit(solution)/shard_map/back/pallas_call | solution.py:1279
  164.1 8.2 %update.1 = (bf16[2048,512]{1,0:T(8,128)(2,1)}, f32[2048,512]{1,0:T(8,128)}, f32[1,1]{1,0:T(1,128)}, f32[16,1536]{1,0:T(8,128)}, f32[16,512]{1,0:T(8,128)}, /*in...) custom-call(f32[8,128]{1,0:T(8,128)} %get-tuple-element.76.total_ref, ...), custom_call_target="tpu_custom_call" | custom-call | tf_op jit(solution)/shard_map/update/pallas_call | solution.py:1370
where the time goes:
time: 173 us; the launch traced here: 172 us
  Pallas kernels  171 us (99%)
    pallas_call x1, Pallas kernels, direct_body(): remote_call(front_kernel, groups, seqs, 'front', 0, [*((hbm, shape, BF) f...  72.8 us
    pallas_call x1, Pallas kernels, direct_body(): remote_call(back_kernel, groups, seqs, 'back', 2, [(hbm, tokens, F32), (v...  59.4 us
    pallas_call x1, Pallas kernels, direct_body(): remote_call(middle_kernel, groups, seqs, 'middle', 1, [(hbm, tokens, F32)...  30.7 us
    pallas_call x1, Pallas kernels, body(): pl.pallas_call(functools.partial(update_kernel, parts), in_specs=[spec(vm...  8.15 us

commit v1 on v0

--- a/solution.py
+++ b/solution.py
@@ -98,7 +98,7 @@
     return jnp.concatenate([near, far], axis=0)
 
 
-def attend_spans(spans, mixed_ref, width, summ_ref, summ_vt_ref, out_ref, lse_ref):
+def attend_spans(spans, mixed_ref, width, summ_ref, summ_vt_ref, out_ref, lse_ref=None, probs_ref=None):
     units = [(pl.ds(row, SPAN), index, caps, pair) for row, index, caps in spans for pair in range(width // LANES)]
     queries, keys, values_t = [], [], []
     for rows, index, caps, pair in units:
@@ -113,17 +113,21 @@
     peaks = [jnp.max(s, axis=0, keepdims=True) for s in scores]
     expos = [jnp.exp(s - p) for s, p in zip(scores, peaks)]
     totals = [jnp.sum(e, axis=0, keepdims=True) for e in expos]
-    expos = [e.astype(BF) for e in expos]
-    outs = [dot(v, e) for v, e in zip(values_t, expos)]
-    outs = [o * (1.0 / t) for o, t in zip(outs, totals)]
-    for (rows, index, caps, pair), out, peak, total in zip(units, outs, peaks, totals):
+    probs = [(e * (1.0 / t)).astype(BF) for e, t in zip(expos, totals)]
+    outs = [dot(v, p) for v, p in zip(values_t, probs)]
+    for (rows, index, caps, pair), out, prob, peak, total in zip(units, outs, probs, peaks, totals):
         at = pair * LANES
         out_ref[rows, at : at + LANES] = fold_heads(out).astype(BF)
-        lse_ref[index, pair : pair + 1, :] = peak + jnp.log(total)
+        if lse_ref is not None:
+            lse_ref[index, pair : pair + 1, :] = peak + jnp.log(total)
+        if probs_ref is not None:
+            at = pair * 4 * SPAN
+            probs_ref[rows, at : at + 2 * SPAN] = prob[:SPAN]
+            probs_ref[rows, at + 2 * SPAN : at + 4 * SPAN] = prob[SPAN:]
 
 
 def attend_back_spans(
-    spans, mixed_ref, grad_ref, width, summ_ref, summ_kt_ref, lse_ref, back_ref, dsumm_ref
+    spans, mixed_ref, grad_ref, width, summ_ref, summ_kt_ref, lse_ref, back_ref, dsumm_ref, probs_ref=None
 ):
     pairs = width // LANES
     units = [(pl.ds(row, SPAN), index, caps, pair) for row, index, caps in spans for pair in range(pairs)]
@@ -137,10 +141,18 @@
         keys.append(jnp.concatenate([near_k, summ_ref[:, at : at + LANES]], axis=0))
         keys_t.append(jnp.concatenate([near_k.T, summ_kt_ref[at : at + LANES, :]], axis=1))
         values.append(jnp.concatenate([near_v, summ_ref[:, width + at : width + at + LANES]], axis=0))
-    scores = [dot_nt(k, q) for k, q in zip(keys, queries)]
-    dprobs = [dot_nt(v, g) for v, g in zip(values, grads)]
-    scores = [mask_scores(s, unit[2]) for s, unit in zip(scores, units)]
-    probs = [jnp.exp(s - lse_ref[index, pair : pair + 1, :]) for s, (_, index, _, pair) in zip(scores, units)]
+    if probs_ref is None:
+        scores = [dot_nt(k, q) for k, q in zip(keys, queries)]
+        dprobs = [dot_nt(v, g) for v, g in zip(values, grads)]
+        scores = [mask_scores(s, unit[2]) for s, unit in zip(scores, units)]
+        probs = [jnp.exp(s - lse_ref[index, pair : pair + 1, :]) for s, (_, index, _, pair) in zip(scores, units)]
+    else:
+        dprobs = [dot_nt(v, g) for v, g in zip(values, grads)]
+        probs = []
+        for rows, _, _, pair in units:
+            at = pair * 4 * SPAN
+            near, far = probs_ref[rows, at : at + 2 * SPAN], probs_ref[rows, at + 2 * SPAN : at + 4 * SPAN]
+            probs.append(jnp.concatenate([near, far], axis=0).astype(F32))
     deltas = [jnp.sum(p * d, axis=0, keepdims=True) for p, d in zip(probs, dprobs)]
     dscores = [(p * (d - delta)).astype(BF) for p, d, delta in zip(probs, dprobs, deltas)]
     probs = [p.astype(BF) for p in probs]
@@ -225,7 +237,7 @@
 
 class Copies:
     def __init__(self, send_sems, recv_sems):
-        self.send, self.recv, self.made = send_sems, recv_sems, []
+        self.send, self.recv, self.made, self.left = send_sems, recv_sems, [], 0
 
     def start(self, src, src_index, dst, dst_index, device):
         at = len(self.made)
@@ -244,8 +256,9 @@
         return self.start(ref, index, ref, index, device)
 
     def finish(self):
-        for copy in self.made:
+        for copy in self.made[self.left :]:
             copy.wait_send()
+        self.left = len(self.made)
 
 
 class Loads:
@@ -422,23 +435,30 @@
     return groups + seqs - 2
 
 
-class Ticker:
-    def __init__(self, *starts):
-        self.waiting, self.time = list(starts), 0
-
-    def __call__(self):
-        for start, steps in reversed(self.waiting):
-            if self.time >= start:
-                next(steps, None)
-        self.time += 1
-
-    def finish(self):
-        run_all(*(steps for _, steps in self.waiting))
-
-
-def tick(*steps):
-    for step in steps:
-        next(step, None)
+def square_sums(value):
+    total = 0.0
+    for at in range(0, value.shape[1], LANES):
+        block = jnp.square(value[:, at : at + LANES])
+        if block.shape[0] < 8:
+            total = total + jnp.concatenate([block, jnp.zeros((8 - block.shape[0], LANES), F32)], axis=0)
+        for row in range(0, block.shape[0] // 8 * 8, 8):
+            total = total + block[row : row + 8]
+    return total
+
+
+class Schedule:
+    def __init__(self, **steps):
+        self.steps = steps
+
+    def __call__(self, *names):
+        for name in names:
+            next(self.steps[name], None)
+
+    def plan(self, *calls):
+        return {at: functools.partial(self, *names.split()) for at, names in enumerate(calls) if names}
+
+    def finish(self, *names):
+        run_all(*(self.steps[name] for name in names or self.steps))
 
 
 def run_all(*steps):
@@ -471,17 +491,19 @@
     fresh_out[...] = master - rate * (update + DECAY * master)
 
 
-def update_kernel(
-    parts, total_ref, qkv_grad, pu_grad, down_grad, norm_grad, outputs_hbm, input_grad_hbm, *refs
-):
-    state, outs, (outputs_ref, input_ref, sems) = refs[:15], refs[15:-3], refs[-3:]
-    outputs_out, input_out, norm_out, moments, squares, fresh = outs[0], outs[1], outs[2], outs[3:8], outs[8:13], outs[13:18]
+def update_kernel(parts, total_ref, norm_grad, *refs):
+    sources, results, held, sems = refs[:20], refs[20:39], refs[39:-1], refs[-1]
+    outputs_ref, input_ref, grad_refs, state, made, wide_ref = held[0], held[1], held[2:5], held[5:20], held[20:35], held[35]
+    outputs_hbm, input_hbm, grads_hbm, state_hbm = sources[0], sources[1], sources[2:5], sources[5:]
     loads = Loads(sems)
-    ways = ((input_grad_hbm, input_ref, input_out), (outputs_hbm, outputs_ref, outputs_out))
-    reads = [Sliced(loads, src, via, parts).start_all() for src, via, _ in ways]
-    stores = [Sliced(loads, via, dst, parts) for _, via, dst in ways]
-    grad_norm = jnp.sqrt(total_ref[0:1, 0:1])
-    norm_out[...] = grad_norm
+    ways = ((input_hbm, input_ref, wide_ref, results[1]), (outputs_hbm, outputs_ref, outputs_ref, results[0]))
+    small = [loads.start(src, via) for src, via in zip((*grads_hbm, *state_hbm), (*grad_refs, *state))]
+    reads = [Sliced(loads, src, via, parts).start_all() for src, via, _, _ in ways]
+    stores = [Sliced(loads, via, dst, parts) for _, _, via, dst in ways]
+    for load in small:
+        load.wait()
+    grad_norm = jnp.sqrt(jnp.sum(total_ref[...], keepdims=True))
+    results[2][...] = grad_norm
     factor = jnp.minimum(1.0, CLIP / (grad_norm + 1e-06))
     width = state[1].shape[1]
     piece = state[4].shape[1]
@@ -489,19 +511,27 @@
     index = lax.axis_index("batch") * lax.axis_size("seq") + lax.axis_index("seq")
     block = norm_grad[:, pl.ds(pl.multiple_of(index // per * LANES, LANES), LANES)]
     own = pltpu.roll(block, (LANES - index % per * piece) % LANES, 1)[:, :piece]
+    qkv_grad, pu_grad, down_grad = grad_refs
     grads = (qkv_grad[...], pu_grad[:, :width], pu_grad[:, width:], down_grad[...], own)
+    results[18][...] = own[3:4] * factor
+    last = []
     for at, (grad, rate) in enumerate(zip(grads, RATES)):
         adam(
             grad * factor, state[at][...], state[5 + at][...], state[10 + at][...], rate,
-            moments[at], squares[at], fresh[at],
+            made[at], made[5 + at], made[10 + at],
         )
-    outs[18][...] = own[3:4] * factor
+        last += [loads.start(made[k], results[3 + k]) for k in (at, 5 + at, 10 + at)]
     for read, store in zip(reads, stores):
         for part in range(parts):
             read.wait(part)
+            if read.dst is input_ref:
+                here = pl.ds(part * read.size, read.size)
+                wide_ref[here, :] = input_ref[here, :].astype(F32)
             store.start(part)
     for store in stores:
         store.wait_all()
+    for store in last:
+        store.wait()
 
 
 def cast_shards(p, seqs, qkv_ref, proj_ref, up_ref, down_ref, norm_ref, qkv_full, pu_full, down_full, norm_full):
@@ -577,7 +607,7 @@
 
 def front_kernel(
     groups, seqs, length_ref, x_hbm, og_hbm, qkv_ref, proj_ref, up_ref, down_ref, norm_ref,
-    qkv_hbm, pu_hbm, down_hbm, norms_out, mixed_hbm, summ_ref, attn_hbm, lse_ref,
+    qkv_hbm, pu_hbm, down_hbm, norms_out, mixed_hbm, summ_ref, attn_hbm, probs_hbm,
     outputs_hbm, resid_hbm, slope_hbm, down_grad_hbm,
     x_ref, og_ref, qkv_full, pu_full, down_full, mixed_ref, attn_ref, outputs_ref, resid_ref, activ_ref, slope_ref,
     down_grad_ref, norm_full, sum_scr, vt_scr, load_sems, send_sems, recv_sems,
@@ -597,14 +627,14 @@
     og_load = loads.start(og_hbm, og_ref)
     copies = Copies(send_sems, recv_sems)
     half_down, half_pu = down_full.shape[3] // 2, pu_full.shape[4] // 2
-    in_kv = fast_gather_steps(p, copies, qkv_full, cols=slice(width, 3 * width))
-    in_norm = gather_steps(p, copies, norm_full)
-    ticker = Ticker(
-        (0, gather_steps(p, copies, qkv_full, cols=slice(0, width))),
-        (1, gather_steps(p, copies, pu_full, cols=slice(0, half_pu))),
-        (2, gather_steps(p, copies, pu_full, cols=slice(half_pu, 2 * half_pu))),
-        (3, gather_steps(p, copies, down_full, rows=slice(0, half_down))),
-        (4, gather_steps(p, copies, down_full, rows=slice(half_down, 2 * half_down))),
+    move = Schedule(
+        kv=fast_gather_steps(p, copies, qkv_full, cols=slice(width, 3 * width)),
+        norm=gather_steps(p, copies, norm_full),
+        q=gather_steps(p, copies, qkv_full, cols=slice(0, width)),
+        pu0=gather_steps(p, copies, pu_full, cols=slice(0, half_pu)),
+        pu1=gather_steps(p, copies, pu_full, cols=slice(half_pu, 2 * half_pu)),
+        down0=gather_steps(p, copies, down_full, rows=slice(0, half_down)),
+        down1=gather_steps(p, copies, down_full, rows=slice(half_down, 2 * half_down)),
     )
     xhat_ref = resid_ref
 
@@ -613,21 +643,10 @@
         x_load.wait(index)
         xhat_ref[here, :] = normalize(x_ref[here, :].astype(F32))[0]
 
-    tick(in_norm, in_kv)
-
-    def first():
-        tick(in_norm, in_kv)
-        ticker()
-
-    def second():
-        tick(in_norm, in_kv)
-
-    def third():
-        tick(in_norm, in_kv)
-        ticker()
-
-    loop(count, center, {0: first, count // 2: second, count - 1: third})
-    tick(in_norm, in_kv)
+    move("norm", "kv")
+    loop(count, center, move.plan("norm kv q pu0", "", "norm kv", "norm kv q pu1"))
+    move("norm", "kv")
+    move("pu0")
     join_norms(norm_full, seqs, LANES // norm_ref.shape[1], norms_out)
     gain, shift = norms_out[0:1, :], norms_out[1:2, :]
 
@@ -647,11 +666,11 @@
                 mixed[part * SPAN : (part + 1) * SPAN], length, (first_span + span) * SPAN
             )
 
-    loop(count, keys_values, {0: ticker, count // 2: ticker})
+    loop(count, keys_values, move.plan("q", "pu1", "q"))
     summ_ref[p.z, p.c] = sum_scr[...].astype(BF)
     along = [copies.push(summ_ref, (p.z, p.c), device) for device in p.along[1:]]
     sib = [copies.push(summ_ref, (p.z, p.c), p.sibling)]
-    ticker()
+    move("q")
     stores = [loads.start(qkv_full, qkv_hbm)]
     mixed_store = Sliced(loads, mixed_ref, mixed_hbm, count)
 
@@ -661,24 +680,29 @@
         mixed_store.start(index)
 
     loop(count, queries)
+    move("pu0")
     for k, copy in enumerate(along, 1):
         copy.wait_recv()
         sib.append(copies.push(summ_ref, (p.before[k], p.c), p.sibling))
     for copy in sib:
         copy.wait_recv()
+    move("pu1", "down0")
     vt_scr[...] = summ_ref[:, :, :, width:].reshape(local * seqs, width).T
     summ_rows = SummaryView(summ_ref, local * seqs)
     attn_store = Sliced(loads, attn_ref, attn_hbm, count)
+    probs_ref = activ_ref
+    probs_store = Sliced(loads, probs_ref, probs_hbm, count)
 
     def attend(index):
         spans = []
         for k in range(per):
             span = index * per + k
             spans.append((pl.multiple_of(span * SPAN, SPAN), span, span_caps(length, first_span + span)))
-        attend_spans(spans, mixed_ref, width, summ_rows, vt_scr, attn_ref, lse_ref)
+        attend_spans(spans, mixed_ref, width, summ_rows, vt_scr, attn_ref, probs_ref=probs_ref)
         attn_store.start(index)
-
-    loop(count, attend, {k: ticker for k in range(1, count, 2)})
+        probs_store.start(index)
+
+    loop(count, attend, move.plan("pu0 down0 down1", "pu1", "pu0 down1", "pu1 down0"))
     gain_two, shift_two = norms_out[2:3, :], norms_out[3:4, :]
     resid_store, slope_store = (
         Sliced(loads, src, dst, count) for src, dst in ((resid_ref, resid_hbm), (slope_ref, slope_hbm))
@@ -691,13 +715,14 @@
         resid_ref[here, :] = resid
         resid_store.start(index)
         normed = (normalize(resid)[0] * gain_two + shift_two).astype(BF)
+        probs_store.wait(index)
         for at in range(0, hidden, chunk):
             value, slope = gelu_parts(dot(normed, columns(pu_full, width + at, chunk)))
             activ_ref[here, at : at + chunk] = value.astype(BF)
             slope_ref[here, at : at + chunk] = slope.astype(BF)
         slope_store.start(index)
 
-    loop(count, expand, {k: ticker for k in range(1, count, 2)})
+    loop(count, expand, move.plan("down1", "down0", "down1"))
     stores.append(loads.start(pu_full, pu_hbm))
     og_load.wait()
     parts = hidden // TILE
@@ -709,7 +734,7 @@
         grad_store.start(index)
 
     loop(parts, down_grad)
-    ticker.finish()
+    move.finish()
     stores.append(loads.start(down_full, down_hbm))
     outputs_store = Sliced(loads, outputs_ref, outputs_hbm, count)
 
@@ -752,19 +777,16 @@
     meet(p)
     copies = Copies(send_sems, recv_sems)
     half = down_out.shape[0] // 2
-    ticker = Ticker(
-        *(
-            (
-                at,
-                scatter_steps(
-                    p, copies, loads, down_grad_hbm.at[:, :, :, half * at : half * (at + 1)], *buffers[5 * at : 5 * at + 5],
-                    down_out.at[half * at : half * (at + 1)],
-                ),
+    move = Schedule(
+        **{
+            f"down{at}": scatter_steps(
+                p, copies, loads, down_grad_hbm.at[:, :, :, half * at : half * (at + 1)], *buffers[5 * at : 5 * at + 5],
+                down_out.at[half * at : half * (at + 1)],
             )
             for at in range(2)
-        )
+        }
     )
-    ticker()
+    move("down0", "down1")
     attn_load = loads.start(attn_hbm, attn_ref)
     norm_grad_ref[...] = jnp.zeros_like(norm_grad_ref)
     resid_grad_store, attn_grad_store = (
@@ -803,7 +825,7 @@
         norm_grad_ref[0:1, :] += jnp.sum(back * xhat, axis=0, keepdims=True)
         norm_grad_ref[1:2, :] += jnp.sum(back, axis=0, keepdims=True)
 
-    loop(count, tile, {k: ticker for k in range(count)})
+    loop(count, tile, move.plan("down0", "down1", "down0", "down1 down0"))
     attn_load.wait()
     pu_grad_ref[:, :width] = dot_tn(attn_ref[...], pig_ref[...]).astype(BF)
 
@@ -811,20 +833,20 @@
         at = pl.multiple_of(width + index * TILE, TILE)
         pu_grad_ref[:, pl.ds(at, TILE)] = dot_tn(normed_ref[...], pre_grad_ref[:, row_block(index, TILE)]).astype(BF)
 
-    loop(hidden // TILE, up_grad, {1: ticker})
+    loop(hidden // TILE, up_grad, move.plan("down1", "", "down0"))
     pu_store = loads.start(pu_grad_ref, pu_grad_hbm)
     resid_grad_store.wait_all()
     attn_grad_store.wait_all()
-    ticker.finish()
+    move.finish()
     pu_store.wait()
     copies.finish()
 
 
 def back_kernel(
-    groups, seqs, length_ref, x_hbm, mixed_hbm, grad_hbm, lse_ref, summ_ref, pu_hbm, resid_grad_hbm, down_ref,
+    groups, seqs, length_ref, x_hbm, mixed_hbm, grad_hbm, probs_hbm, summ_ref, pu_hbm, resid_grad_hbm, down_ref,
     norms_ref, weight_hbm, norm_two_ref,
     input_grad_hbm, qkv_out, pu_out, norm_out, total_out,
-    x_ref, mixed_ref, grad_ref, resid_grad_ref, weight_ref, input_grad_ref,
+    x_ref, mixed_ref, grad_ref, probs_ref, resid_grad_ref, weight_ref, input_low_ref,
     mg_scr, xhat_ref, kt_scr, dsumm_scr, dsumm_got, dsumm_low, dsumm_last, extra_scr, q_grad, k_grad, v_grad,
     gain_cols, shift_cols,
     *scratch,
@@ -839,7 +861,8 @@
     group = 2
     count, steps = rows // TILE, local // group
     reads = [
-        Sliced(loads, src, dst, steps) for src, dst in ((mixed_hbm, mixed_ref), (grad_hbm, grad_ref))
+        Sliced(loads, src, dst, steps)
+        for src, dst in ((mixed_hbm, mixed_ref), (grad_hbm, grad_ref), (probs_hbm, probs_ref))
     ]
     for index in range(2):
         for read in reads:
@@ -851,11 +874,14 @@
         return scatter_steps(p, copies, loads, grad, *buffers[5 * at : 5 * at + 5], out)
 
     half = pu_hbm.shape[4] // 2
-    ticker = Ticker(
-        *((at, scatter(pu_hbm.at[:, :, :, :, half * at : half * (at + 1)], at, pu_out.at[:, half * at : half * (at + 1)]))
-          for at in range(2))
+    outs = [qkv_out.at[:, width * at : width * (at + 1)] for at in range(3)]
+    move = Schedule(
+        pu0=scatter(pu_hbm.at[:, :, :, :, :half], 0, pu_out.at[:, :half]),
+        pu1=scatter(pu_hbm.at[:, :, :, :, half:], 1, pu_out.at[:, half:]),
+        q=scatter(q_grad, 2, outs[0]), k=scatter(k_grad, 3, outs[1]), v=scatter(v_grad, 4, outs[2]),
+        norm=share_sum_steps(p, copies, norm_mine, along_norm, across_norm, norm_out),
     )
-    ticker()
+    move("pu0", "pu1")
     late = [loads.start(src, dst) for src, dst in ((x_hbm, x_ref), (weight_hbm, weight_ref))]
     resid_grad_load = loads.start(resid_grad_hbm, resid_grad_ref)
     kt_scr[...] = summ_ref[:, :width].T
@@ -868,10 +894,10 @@
         each = []
         for k in range(group):
             span = index * group + k
-            each.append((pl.multiple_of(span * SPAN, SPAN), span, span_caps(length, first_span + span)))
-        attend_back_spans(each, mixed_ref, grad_ref, width, summ_ref, kt_scr, lse_ref, mg_scr, dsumm_scr)
-
-    loop(steps, attend_back, {at: ticker for at in range(0, steps, 2)})
+            each.append((pl.multiple_of(span * SPAN, SPAN), span, None))
+        attend_back_spans(each, mixed_ref, grad_ref, width, summ_ref, kt_scr, None, mg_scr, dsumm_scr, probs_ref)
+
+    loop(steps, attend_back, move.plan("pu0", "", "pu1", "pu0", "", "pu1 pu0", "", "pu1"))
     swap = []
     for z in range(p.chips):
         block = pl.ds(pl.multiple_of((2 * z + p.other) * local, local), local)
@@ -920,19 +946,10 @@
         norm_mine[1:2, :] = shift_sums + (norm_mine[1:2, :] if at else 0.0)
 
     norm_mine[2:4, :] = norm_two_ref[...]
-    outs = [qkv_out.at[:, width * at : width * (at + 1)] for at in range(3)]
     weight_grad(q_grad, 0)
-    out_q = scatter(q_grad, 2, outs[0])
-    tick(out_q)
-    ticker()
-
-    def back_q(index):
-        here = row_block(index, TILE)
-        input_grad_ref[here, :] = dot_nt(mg_scr[here, :width], weight_ref[:, :width])
-
-    loop(count, back_q)
-    tick(out_q)
-    ticker()
+    move("q", "pu0")
+
+    move("pu1")
     total = half_sum(p.z)
     for k, copy in enumerate(along):
         copy.wait_recv()
@@ -949,34 +966,27 @@
 
     loop(local // 2, add_extra)
     weight_grad(k_grad, 1)
-    out_k = scatter(k_grad, 3, outs[1])
-    tick(out_k, out_q)
+    move("k", "q")
     weight_grad(v_grad, 2)
-    out_v = scatter(v_grad, 4, outs[2])
-    norm_sum = share_sum_steps(p, copies, norm_mine, along_norm, across_norm, norm_out)
-    tick(out_v, norm_sum, out_k, out_q)
-    ticker()
+    move("v", "norm", "k", "q")
     resid_grad_load.wait()
-    store = Sliced(loads, input_grad_ref, input_grad_hbm, count)
+    store = Sliced(loads, input_low_ref, input_grad_hbm, count)
 
     def finish(index):
         here = row_block(index, TILE)
         xhat, rstd = normalize(x_ref[here, :].astype(F32))
-        back = input_grad_ref[here, :] + dot_nt(mg_scr[here, width:], weight_ref[:, width:])
-        input_grad_ref[here, :] = resid_grad_ref[here, :] + norm_back(back, gain, xhat, rstd)
+        back = dot_nt(mg_scr[here, :], weight_ref[...])
+        input_low_ref[here, :] = (resid_grad_ref[here, :] + norm_back(back, gain, xhat, rstd)).astype(BF)
         store.start(index)
 
-    def advance():
-        tick(out_v, norm_sum, out_k, out_q)
-        ticker()
-
-    loop(count, finish, {k: advance for k in range(0, count, 2)})
-    run_all(out_v, norm_sum, out_k, out_q)
-    ticker.finish()
-    local_sum = sum(jnp.sum(jnp.square(out[...]), keepdims=True) for out in (qkv_out, pu_out, down_ref))
-    sq_mine[...] = jnp.broadcast_to(local_sum, sq_mine.shape)
+    loop(count, finish, move.plan("v k", "v norm q", "k", "v"))
+    sq_mine[...] = square_sums(pu_out[...]) + square_sums(down_ref[...])
+    move("k", "q", "norm")
+    copies.finish()
+    move.finish()
+    sq_mine[...] += square_sums(qkv_out[...])
     run_all(share_sum_steps(p, copies, sq_mine, along_sq, across_sq, total_out))
-    total_out[...] = total_out[...] + jnp.sum(jnp.square(norm_out[...]), keepdims=True)
+    total_out[...] += square_sums(norm_out[...])
     store.wait_all()
     copies.finish()
 
@@ -1180,7 +1190,7 @@
     norm_total = lax.psum(norm_grad, ("batch", "seq"))
     squares = lax.psum(sum(jnp.sum(grad * grad) for grad in reduced), ("batch", "seq"))
     squares = squares + jnp.sum(norm_total * norm_total)
-    return (*reduced, norm_total, jnp.broadcast_to(squares, (8, LANES)))
+    return (*reduced, norm_total, jnp.zeros((8, LANES), F32).at[0, 0].set(squares))
 
 
 def mlp_call(x, attn_out, grad_rows, norms, pu_full, down_full):
@@ -1227,12 +1237,12 @@
     )
     tokens = (rows, width)
     (
-        qkv_full, pu_full, down_full, norms, mixed, summ, attn_out, lse, outputs, resid, slope, down_grad,
+        qkv_full, pu_full, down_full, norms, mixed, summ, attn_out, probs, outputs, resid, slope, down_grad,
     ) = remote_call(
         front_kernel, groups, seqs, "front", 0,
         [
             *((hbm, shape, BF) for shape in shapes), (vmem, (4, width), F32), (hbm, (rows, 3 * width), BF),
-            (vmem, (chips, 2, local, 2 * width), BF), (hbm, tokens, BF), (vmem, (local, pairs, 2 * SPAN), F32),
+            (vmem, (chips, 2, local, 2 * width), BF), (hbm, tokens, BF), (hbm, (rows, 4 * SPAN * pairs), BF),
             (hbm, tokens, BF), (hbm, tokens, F32), (hbm, (rows, hidden), BF), (hbm, (hidden, width), BF),
         ],
         [smem, hbm, hbm] + [vmem] * 5,
@@ -1242,7 +1252,7 @@
             vmem((rows, hidden), BF), vmem((rows, hidden), BF), vmem((hidden, width), BF),
             vmem((*grid3, 4, LANES), F32), vmem((local, 2 * width), F32), vmem((width, spans), BF),
         ],
-        4 + 6 * count + hidden // TILE, 6 * GATHER_COPIES + fast_gather_copies(chips) + 2 * chips,
+        4 + 7 * count + hidden // TILE, 6 * GATHER_COPIES + fast_gather_copies(chips) + 2 * chips,
     )(lengths, x, grad_rows, *state[:5])
     pu_flat, down_flat = pu_full.reshape(width, width + hidden), down_full.reshape(hidden, width)
     resid_grad, attn_grad, pu_grad, down_own, norm_two = remote_call(
@@ -1264,8 +1274,8 @@
     blocks = ((own_rows, half),) * 2 + ((own_rows, width),) * 3
     summ_block = (local, 2 * width)
     scratch = [
-        vmem(tokens, BF), vmem((rows, 3 * width), BF), vmem(tokens, BF), vmem(tokens, F32),
-        vmem((width, 3 * width), BF), vmem(tokens, F32),
+        vmem(tokens, BF), vmem((rows, 3 * width), BF), vmem(tokens, BF), vmem(probs.shape, BF), vmem(tokens, F32),
+        vmem((width, 3 * width), BF), vmem(tokens, BF),
         vmem((rows, 3 * width), BF), vmem(tokens, BF), vmem((width, spans), BF), vmem((spans, 2 * width), F32),
         vmem((chips, *summ_block), F32), vmem((chips - 1, *summ_block), BF),
         vmem((chips - 1, *summ_block), BF), vmem(summ_block, F32),
@@ -1279,14 +1289,14 @@
     input_grad, qkv_own, pu_own, norm_total, total = remote_call(
         back_kernel, groups, seqs, "back", 2,
         [
-            (hbm, tokens, F32), (vmem, (own_rows, 3 * width), F32), (vmem, (own_rows, width + hidden), F32),
+            (hbm, tokens, BF), (vmem, (own_rows, 3 * width), F32), (vmem, (own_rows, width + hidden), F32),
             (vmem, (4, width), F32), (vmem, (8, LANES), F32),
         ],
-        [smem, hbm, hbm, hbm, vmem, vmem, hbm, hbm, vmem, vmem, hbm, vmem],
-        scratch, local + 3 + 5 + count,
+        [smem, hbm, hbm, hbm, hbm, vmem, hbm, hbm, vmem, vmem, hbm, vmem],
+        scratch, 3 * local // 2 + 3 + 5 + count,
         5 * SCATTER_COPIES + 2 * share_copies(groups, seqs) + 2 * chips,
     )(
-        lengths, x, mixed, attn_grad, lse, summ.reshape(spans, 2 * width), pu_grad.reshape(shapes[1]),
+        lengths, x, mixed, attn_grad, probs, summ.reshape(spans, 2 * width), pu_grad.reshape(shapes[1]),
         resid_grad, down_own, norms, qkv_full.reshape(width, 3 * width), norm_two,
     )
     return outputs, input_grad, (qkv_own, pu_own, down_own), norm_total, total
@@ -1359,28 +1369,31 @@
 
 def body(groups, seqs, *args):
     state = args[3:]
-    direct = groups == 4 and seqs % 4 == 0 and state[0].shape[0] % 16 == 0 and args[0].shape[1] % TILE == 0
+    rows, width = args[0].shape[1:]
+    direct = groups == 4 and seqs % 4 == 0 and state[0].shape[0] % 16 == 0 and rows % TILE == 0
+    direct = direct and rows // SPAN * seqs == SPAN and state[2].shape[1] == 4 * SPAN * (width // LANES)
     run = direct_body if direct else plain_body
     outputs, input_grad, grads, norm_total, total = run(groups, seqs, *args)
+    input_grad = input_grad.astype(BF)
     sds = jax.ShapeDtypeStruct
     vmem, hbm = pltpu.VMEM, pl.ANY
     spec = lambda space: pl.BlockSpec(memory_space=space)
     held = [sds(w.shape, F32) for w in state[:5]]
     parts = 8
+    operands = (outputs, input_grad, *grads, *state)
     outputs, input_grad, grad_norm, *fresh, shift_clipped = pl.pallas_call(
         functools.partial(update_kernel, parts),
-        in_specs=[spec(vmem)] * 5 + [spec(hbm)] * 2 + [spec(vmem)] * 15,
-        out_specs=[spec(hbm)] * 2 + [spec(vmem)] * 17,
+        in_specs=[spec(vmem)] * 2 + [spec(hbm)] * 20,
+        out_specs=[spec(hbm)] * 2 + [spec(vmem)] + [spec(hbm)] * 15 + [spec(vmem)],
         out_shape=[
-            sds(outputs.shape, BF), sds(input_grad.shape, F32), sds((1, 1), F32), *held * 3,
+            sds(outputs.shape, BF), sds(outputs.shape, F32), sds((1, 1), F32), *held * 3,
             sds((1, state[4].shape[1]), F32),
         ],
-        scratch_shapes=[
-            vmem(outputs.shape, BF), vmem(input_grad.shape, F32), pltpu.SemaphoreType.DMA((4 * parts,)),
-        ],
+        scratch_shapes=[vmem(a.shape, a.dtype) for a in operands]
+        + [vmem(w.shape, F32) for w in held * 3] + [vmem(outputs.shape, F32), pltpu.SemaphoreType.DMA((4 * parts + 33,))],
         compiler_params=PARAMS,
         name="update",
-    )(total, *grads, norm_total, outputs, input_grad, *state)
+    )(total, norm_total, *operands)
     return (outputs[None], input_grad[None], grad_norm[0, 0], *fresh, shift_clipped[0])
 
 

time: 173 us -> 160 us (0.925)
  Pallas kernels: 171 us -> 158 us
    pallas_call x1, Pallas kernels: 59.4 us -> 53.8 us  [direct_body(): remote_call(back_kernel, groups, seqs, 'back', 2, [(hbm, tokens, BF), (vm...]
    pallas_call x1, Pallas kernels: 30.7 us -> 27.1 us  [direct_body(): remote_call(middle_kernel, groups, seqs, 'middle', 1, [(hbm, tokens, F32)...]
    pallas_call x1, Pallas kernels: 72.8 us -> 70.3 us  [direct_body(): remote_call(front_kernel, groups, seqs, 'front', 0, [*((hbm, shape, BF) f...]
where the time goes in v1:
time: 160 us; the launch traced here: 159 us
  Pallas kernels  158 us (99%)
    pallas_call x1, Pallas kernels, direct_body(): remote_call(front_kernel, groups, seqs, 'front', 0, [*((hbm, shape, BF) f...  70.3 us
    pallas_call x1, Pallas kernels, direct_body(): remote_call(back_kernel, groups, seqs, 'back', 2, [(hbm, tokens, BF), (vm...  53.8 us
    pallas_call x1, Pallas kernels, direct_body(): remote_call(middle_kernel, groups, seqs, 'middle', 1, [(hbm, tokens, F32)...  27.1 us
    pallas_call x1, Pallas kernels, body(): pl.pallas_call(functools.partial(update_kernel, parts), in_specs=[spec(vm...  6.6 us

profile of v1, /device:TPU:0, one launch (start us, length us, event | category | flops | bytes accessed | tf_op | source)
XLA Modules:
  0.0 159.3 jit_solution(2782511574602928099)
XLA Ops:
  1.3 70.3 %front.1 = (bf16[4,4,2,16,1536]{4,3,2,1,0:T(8,128)(2,1)}, bf16[4,4,2,16,2560]{4,3,2,1,0:T(8,128)(2,1)}, bf16[4,4,2,64,512]{4,3,2,1,0:T(8,128)(2,1)}, f32[4,512]{...) custom-call(s32[1]{0:T(128)S(6)} %copy.37.length_ref, ...), custom_call_target="tpu_custom_call" | custom-call | tf_op jit(solution)/shard_map/front/pallas_call | solution.py:1241
  71.6 27.1 %middle.1 = (f32[2048,512]{1,0:T(8,128)}, bf16[2048,512]{1,0:T(8,128)(2,1)}, bf16[512,2560]{1,0:T(8,128)(2,1)}, f32[64,512]{1,0:T(8,128)}, f32[2,512]{1,0:T(2,128)}) custom-call(bf16[2048,512]{1,0:T(8,128)(2,1)} %bitcast.15, f32[2048,512]{1,0:T(8,128)} %get-tuple-element.61.resid_hbm, bf16[2048,2048]{1,0:T(8,128)(2,1)} %get-tuple-element.62.slope_hbm, ...), custom_call_target="tpu_custom_call" | custom-call | tf_op jit(solution)/shard_map/middle/pallas_call | solution.py:1258
  98.7 53.8 %back.1 = (bf16[2048,512]{1,0:T(8,128)(2,1)}, f32[16,1536]{1,0:T(8,128)}, f32[16,2560]{1,0:T(8,128)}, f32[4,512]{1,0:T(4,128)}, f32[8,128]{1,0:T(8,128)}) custom-call(s32[1]{0:T(128)S(6)} %copy.37.length_ref, bf16[2048,512]{1,0:T(8,128)(2,1)} %bitcast.13, bf16[2048,1536]{1,0:T(8,128)(2,1)} %get-tuple-element.60.mixed_hbm, ...), custom_call_target="tpu_custom_call" | custom-call | tf_op jit(solution)/shard_map/back/pallas_call | solution.py:1289
  152.5 6.6 %update.1 = (bf16[2048,512]{1,0:T(8,128)(2,1)}, f32[2048,512]{1,0:T(8,128)}, f32[1,1]{1,0:T(1,128)}, f32[16,1536]{1,0:T(8,128)}, f32[16,512]{1,0:T(8,128)}, /*in...) custom-call(f32[8,128]{1,0:T(8,128)} %get-tuple-element.76.total_ref, ...), custom_call_target="tpu_custom_call" | custom-call | tf_op jit(solution)/shard_map/update/pallas_call | solution.py:1384

commit v2 on v1

--- a/solution.py
+++ b/solution.py
@@ -608,8 +608,8 @@
 def front_kernel(
     groups, seqs, length_ref, x_hbm, og_hbm, qkv_ref, proj_ref, up_ref, down_ref, norm_ref,
     qkv_hbm, pu_hbm, down_hbm, norms_out, mixed_hbm, summ_ref, attn_hbm, probs_hbm,
-    outputs_hbm, resid_hbm, slope_hbm, down_grad_hbm,
-    x_ref, og_ref, qkv_full, pu_full, down_full, mixed_ref, attn_ref, outputs_ref, resid_ref, activ_ref, slope_ref,
+    activ_hbm, resid_hbm, slope_hbm, down_grad_hbm,
+    x_ref, og_ref, qkv_full, pu_full, down_full, mixed_ref, attn_ref, resid_ref, activ_ref, slope_ref,
     down_grad_ref, norm_full, sum_scr, vt_scr, load_sems, send_sems, recv_sems,
 ):
     p = Place(groups, seqs)
@@ -666,10 +666,14 @@
                 mixed[part * SPAN : (part + 1) * SPAN], length, (first_span + span) * SPAN
             )
 
-    loop(count, keys_values, move.plan("q", "pu1", "q"))
+    loop(count, keys_values, move.plan("q", "pu1 down0", "q"))
     summ_ref[p.z, p.c] = sum_scr[...].astype(BF)
     along = [copies.push(summ_ref, (p.z, p.c), device) for device in p.along[1:]]
     sib = [copies.push(summ_ref, (p.z, p.c), p.sibling)]
+    move("down1", "pu0")
+    for k, copy in enumerate(along, 1):
+        copy.wait_recv()
+        sib.append(copies.push(summ_ref, (p.before[k], p.c), p.sibling))
     move("q")
     stores = [loads.start(qkv_full, qkv_hbm)]
     mixed_store = Sliced(loads, mixed_ref, mixed_hbm, count)
@@ -680,13 +684,9 @@
         mixed_store.start(index)
 
     loop(count, queries)
-    move("pu0")
-    for k, copy in enumerate(along, 1):
-        copy.wait_recv()
-        sib.append(copies.push(summ_ref, (p.before[k], p.c), p.sibling))
+    move("pu1")
     for copy in sib:
         copy.wait_recv()
-    move("pu1", "down0")
     vt_scr[...] = summ_ref[:, :, :, width:].reshape(local * seqs, width).T
     summ_rows = SummaryView(summ_ref, local * seqs)
     attn_store = Sliced(loads, attn_ref, attn_hbm, count)
@@ -702,10 +702,11 @@
         attn_store.start(index)
         probs_store.start(index)
 
-    loop(count, attend, move.plan("pu0 down0 down1", "pu1", "pu0 down1", "pu1 down0"))
+    loop(count, attend, move.plan("pu0 down0", "pu1 down1", "pu0", "pu1"))
     gain_two, shift_two = norms_out[2:3, :], norms_out[3:4, :]
-    resid_store, slope_store = (
-        Sliced(loads, src, dst, count) for src, dst in ((resid_ref, resid_hbm), (slope_ref, slope_hbm))
+    resid_store, slope_store, activ_store = (
+        Sliced(loads, src, dst, count)
+        for src, dst in ((resid_ref, resid_hbm), (slope_ref, slope_hbm), (activ_ref, activ_hbm))
     )
     chunk = 256
 
@@ -721,8 +722,9 @@
             activ_ref[here, at : at + chunk] = value.astype(BF)
             slope_ref[here, at : at + chunk] = slope.astype(BF)
         slope_store.start(index)
-
-    loop(count, expand, move.plan("down1", "down0", "down1"))
+        activ_store.start(index)
+
+    loop(count, expand, move.plan("down0", "down1", "down0", "down1"))
     stores.append(loads.start(pu_full, pu_hbm))
     og_load.wait()
     parts = hidden // TILE
@@ -736,16 +738,7 @@
     loop(parts, down_grad)
     move.finish()
     stores.append(loads.start(down_full, down_hbm))
-    outputs_store = Sliced(loads, outputs_ref, outputs_hbm, count)
-
-    def contract(index):
-        here = row_block(index, TILE)
-        out = resid_ref[here, :] + dot(activ_ref[here, :], down_full[...].reshape(hidden, width))
-        outputs_ref[here, :] = out.astype(BF)
-        outputs_store.start(index)
-
-    loop(count, contract)
-    for store in (mixed_store, attn_store, resid_store, slope_store, grad_store, outputs_store):
+    for store in (mixed_store, attn_store, resid_store, slope_store, activ_store, grad_store):
         store.wait_all()
     for store in stores:
         store.wait()
@@ -844,9 +837,9 @@
 
 def back_kernel(
     groups, seqs, length_ref, x_hbm, mixed_hbm, grad_hbm, probs_hbm, summ_ref, pu_hbm, resid_grad_hbm, down_ref,
-    norms_ref, weight_hbm, norm_two_ref,
-    input_grad_hbm, qkv_out, pu_out, norm_out, total_out,
-    x_ref, mixed_ref, grad_ref, probs_ref, resid_grad_ref, weight_ref, input_low_ref,
+    norms_ref, weight_hbm, norm_two_ref, activ_hbm, resid_hbm, down_hbm,
+    input_grad_hbm, outputs_hbm, qkv_out, pu_out, norm_out, total_out,
+    x_ref, mixed_ref, grad_ref, probs_ref, resid_grad_ref, weight_ref, input_low_ref, resid_ref, down_full_ref, outputs_ref,
     mg_scr, xhat_ref, kt_scr, dsumm_scr, dsumm_got, dsumm_low, dsumm_last, extra_scr, q_grad, k_grad, v_grad,
     gain_cols, shift_cols,
     *scratch,
@@ -880,6 +873,7 @@
         pu1=scatter(pu_hbm.at[:, :, :, :, half:], 1, pu_out.at[:, half:]),
         q=scatter(q_grad, 2, outs[0]), k=scatter(k_grad, 3, outs[1]), v=scatter(v_grad, 4, outs[2]),
         norm=share_sum_steps(p, copies, norm_mine, along_norm, across_norm, norm_out),
+        squares=share_sum_steps(p, copies, sq_mine, along_sq, across_sq, total_out),
     )
     move("pu0", "pu1")
     late = [loads.start(src, dst) for src, dst in ((x_hbm, x_ref), (weight_hbm, weight_ref))]
@@ -897,13 +891,15 @@
             each.append((pl.multiple_of(span * SPAN, SPAN), span, None))
         attend_back_spans(each, mixed_ref, grad_ref, width, summ_ref, kt_scr, None, mg_scr, dsumm_scr, probs_ref)
 
-    loop(steps, attend_back, move.plan("pu0", "", "pu1", "pu0", "", "pu1 pu0", "", "pu1"))
+    loop(steps, attend_back, move.plan("", "pu0", "", "pu1", "pu0", "", "pu1"))
+    activ_ref = probs_ref
+    late += [loads.start(*ends) for ends in ((activ_hbm, activ_ref), (resid_hbm, resid_ref), (down_hbm, down_full_ref))]
     swap = []
     for z in range(p.chips):
         block = pl.ds(pl.multiple_of((2 * z + p.other) * local, local), local)
         swap.append(copies.start(dsumm_scr, block, dsumm_got, z, p.sibling))
     gain, shift = norms_ref[0:1, :], norms_ref[1:2, :]
-    for read in late:
+    for read in late[:2]:
         read.wait()
 
     def recompute(index):
@@ -979,15 +975,28 @@
         input_low_ref[here, :] = (resid_grad_ref[here, :] + norm_back(back, gain, xhat, rstd)).astype(BF)
         store.start(index)
 
-    loop(count, finish, move.plan("v k", "v norm q", "k", "v"))
+    loop(count, finish, move.plan("v k", "norm q", "v k pu0", "v pu1"))
+    for read in late[2:]:
+        read.wait()
+    outputs_store = Sliced(loads, outputs_ref, outputs_hbm, count)
+
+    def contract(index):
+        here = row_block(index, TILE)
+        out = resid_ref[here, :] + dot(activ_ref[here, :], down_full_ref[...])
+        outputs_ref[here, :] = out.astype(BF)
+        outputs_store.start(index)
+
+    loop(count // 2, contract, move.plan("k norm q"))
     sq_mine[...] = square_sums(pu_out[...]) + square_sums(down_ref[...])
-    move("k", "q", "norm")
     copies.finish()
-    move.finish()
+    move.finish("pu0", "pu1", "q", "k", "v", "norm")
     sq_mine[...] += square_sums(qkv_out[...])
-    run_all(share_sum_steps(p, copies, sq_mine, along_sq, across_sq, total_out))
+    move("squares")
+    loop(count // 2, lambda index: contract(index + count // 2), move.plan("squares"))
+    move.finish("squares")
     total_out[...] += square_sums(norm_out[...])
     store.wait_all()
+    outputs_store.wait_all()
     copies.finish()
 
 
@@ -1237,18 +1246,18 @@
     )
     tokens = (rows, width)
     (
-        qkv_full, pu_full, down_full, norms, mixed, summ, attn_out, probs, outputs, resid, slope, down_grad,
+        qkv_full, pu_full, down_full, norms, mixed, summ, attn_out, probs, activ, resid, slope, down_grad,
     ) = remote_call(
         front_kernel, groups, seqs, "front", 0,
         [
             *((hbm, shape, BF) for shape in shapes), (vmem, (4, width), F32), (hbm, (rows, 3 * width), BF),
             (vmem, (chips, 2, local, 2 * width), BF), (hbm, tokens, BF), (hbm, (rows, 4 * SPAN * pairs), BF),
-            (hbm, tokens, BF), (hbm, tokens, F32), (hbm, (rows, hidden), BF), (hbm, (hidden, width), BF),
+            (hbm, (rows, hidden), BF), (hbm, tokens, F32), (hbm, (rows, hidden), BF), (hbm, (hidden, width), BF),
         ],
         [smem, hbm, hbm] + [vmem] * 5,
         [
             vmem(tokens, BF), vmem(tokens, BF), *(vmem(shape, BF) for shape in shapes),
-            vmem((rows, 3 * width), BF), vmem(tokens, BF), vmem(tokens, BF), vmem(tokens, F32),
+            vmem((rows, 3 * width), BF), vmem(tokens, BF), vmem(tokens, F32),
             vmem((rows, hidden), BF), vmem((rows, hidden), BF), vmem((hidden, width), BF),
             vmem((*grid3, 4, LANES), F32), vmem((local, 2 * width), F32), vmem((width, spans), BF),
         ],
@@ -1275,7 +1284,7 @@
     summ_block = (local, 2 * width)
     scratch = [
         vmem(tokens, BF), vmem((rows, 3 * width), BF), vmem(tokens, BF), vmem(probs.shape, BF), vmem(tokens, F32),
-        vmem((width, 3 * width), BF), vmem(tokens, BF),
+        vmem((width, 3 * width), BF), vmem(tokens, BF), vmem(tokens, F32), vmem(down_flat.shape, BF), vmem(tokens, BF),
         vmem((rows, 3 * width), BF), vmem(tokens, BF), vmem((width, spans), BF), vmem((spans, 2 * width), F32),
         vmem((chips, *summ_block), F32), vmem((chips - 1, *summ_block), BF),
         vmem((chips - 1, *summ_block), BF), vmem(summ_block, F32),
@@ -1286,18 +1295,18 @@
         vmem((4, width), F32), vmem((seqs, 4, width), F32), vmem((groups, 4, width), F32),
         vmem((8, LANES), F32), vmem((seqs, 8, LANES), F32), vmem((groups, 8, LANES), F32),
     ]
-    input_grad, qkv_own, pu_own, norm_total, total = remote_call(
+    input_grad, outputs, qkv_own, pu_own, norm_total, total = remote_call(
         back_kernel, groups, seqs, "back", 2,
         [
-            (hbm, tokens, BF), (vmem, (own_rows, 3 * width), F32), (vmem, (own_rows, width + hidden), F32),
-            (vmem, (4, width), F32), (vmem, (8, LANES), F32),
+            (hbm, tokens, BF), (hbm, tokens, BF), (vmem, (own_rows, 3 * width), F32),
+            (vmem, (own_rows, width + hidden), F32), (vmem, (4, width), F32), (vmem, (8, LANES), F32),
         ],
-        [smem, hbm, hbm, hbm, hbm, vmem, hbm, hbm, vmem, vmem, hbm, vmem],
-        scratch, 3 * local // 2 + 3 + 5 + count,
+        [smem, hbm, hbm, hbm, hbm, vmem, hbm, hbm, vmem, vmem, hbm, vmem, hbm, hbm, hbm],
+        scratch, 3 * local // 2 + 6 + 5 + 2 * count,
         5 * SCATTER_COPIES + 2 * share_copies(groups, seqs) + 2 * chips,
     )(
         lengths, x, mixed, attn_grad, probs, summ.reshape(spans, 2 * width), pu_grad.reshape(shapes[1]),
-        resid_grad, down_own, norms, qkv_full.reshape(width, 3 * width), norm_two,
+        resid_grad, down_own, norms, qkv_full.reshape(width, 3 * width), norm_two, activ, resid, down_flat,
     )
     return outputs, input_grad, (qkv_own, pu_own, down_own), norm_total, total
 

time: 160 us -> 152 us (0.950)
  Pallas kernels: 158 us -> 150 us
    pallas_call x1, Pallas kernels: 53.8 us -> 49.4 us  [direct_body(): remote_call(back_kernel, groups, seqs, 'back', 2, [(hbm, tokens, BF), (hb...]
    pallas_call x1, Pallas kernels: 70.3 us -> 66.4 us  [direct_body(): remote_call(front_kernel, groups, seqs, 'front', 0, [*((hbm, shape, BF) f...]
where the time goes in v2:
time: 152 us
  Pallas kernels  150 us (99%)
    pallas_call x1, Pallas kernels, direct_body(): remote_call(front_kernel, groups, seqs, 'front', 0, [*((hbm, shape, BF) f...  66.4 us
    pallas_call x1, Pallas kernels, direct_body(): remote_call(back_kernel, groups, seqs, 'back', 2, [(hbm, tokens, BF), (hb...  49.4 us
    pallas_call x1, Pallas kernels, direct_body(): remote_call(middle_kernel, groups, seqs, 'middle', 1, [(hbm, tokens, F32)...  27.8 us
    pallas_call x1, Pallas kernels, body(): pl.pallas_call(functools.partial(update_kernel, parts), in_specs=[spec(vm...  6.6 us

profile of v2, /device:TPU:0, one launch (start us, length us, event | category | flops | bytes accessed | tf_op | source)
XLA Modules:
  0.0 151.6 jit_solution(16782314942283921412)
XLA Ops:
  1.3 66.4 %front.1 = (bf16[4,4,2,16,1536]{4,3,2,1,0:T(8,128)(2,1)}, bf16[4,4,2,16,2560]{4,3,2,1,0:T(8,128)(2,1)}, bf16[4,4,2,64,512]{4,3,2,1,0:T(8,128)(2,1)}, f32[4,512]{...) custom-call(s32[1]{0:T(128)S(6)} %copy.37.length_ref, ...), custom_call_target="tpu_custom_call" | custom-call | tf_op jit(solution)/shard_map/front/pallas_call | solution.py:1250
  67.7 27.8 %middle.1 = (f32[2048,512]{1,0:T(8,128)}, bf16[2048,512]{1,0:T(8,128)(2,1)}, bf16[512,2560]{1,0:T(8,128)(2,1)}, f32[64,512]{1,0:T(8,128)}, f32[2,512]{1,0:T(2,128)}) custom-call(bf16[2048,512]{1,0:T(8,128)(2,1)} %bitcast.17, f32[2048,512]{1,0:T(8,128)} %get-tuple-element.62.resid_hbm, bf16[2048,2048]{1,0:T(8,128)(2,1)} %get-tuple-element.63.slope_hbm, ...), custom_call_target="tpu_custom_call" | custom-call | tf_op jit(solution)/shard_map/middle/pallas_call | solution.py:1267
  95.5 49.4 %back.1 = (bf16[2048,512]{1,0:T(8,128)(2,1)}, bf16[2048,512]{1,0:T(8,128)(2,1)}, f32[16,1536]{1,0:T(8,128)}, f32[16,2560]{1,0:T(8,128)}, f32[4,512]{1,0:T(4,128)}, /*index=5*/f32[8,128]{1,0:T(8,128)}) custom-call(s32[1]{0:T(128)S(6)} %copy.37.length_ref, bf16[2048,512]{1,0:T(8,128)(2,1)} %bitcast.13, bf16[2048,1536]{1,0:T(8,128)(2,1)} %get-tuple-element.61.mixed_hbm, ...), custom_call_target="tpu_custom_call" | custom-call | tf_op jit(solution)/shard_map/back/pallas_call | solution.py:1298
  144.9 6.6 %update.1 = (bf16[2048,512]{1,0:T(8,128)(2,1)}, f32[2048,512]{1,0:T(8,128)}, f32[1,1]{1,0:T(1,128)}, f32[16,1536]{1,0:T(8,128)}, f32[16,512]{1,0:T(8,128)}, /*in...) custom-call(f32[8,128]{1,0:T(8,128)} %get-tuple-element.78.total_ref, ...), custom_call_target="tpu_custom_call" | custom-call | tf_op jit(solution)/shard_map/update/pallas_call | solution.py:1393

commit v3 on v2

--- a/solution.py
+++ b/solution.py
@@ -314,41 +314,42 @@
     def push(b, k, device):
         return copies.push(full, (b, p.before[k], p.c, rows, cols), device)
 
+    def pass_over(b):
+        sib.append(copies.push(full, (b, slice(None), p.c, rows, cols), p.sibling))
+
     along = [push(p.b, 0, device) for device in p.along[1:]]
-    to_x, to_y, sib = [push(p.b, 0, p.x)], [push(p.b, 0, p.y)], [push(p.b, 0, p.sibling)]
+    to_x, to_y, sib = [push(p.b, 0, p.x)], [push(p.b, 0, p.y)], []
     yield
     for k, copy in enumerate(along, 1):
         copy.wait_recv()
         to_x.append(push(p.b, k, p.x))
         to_y.append(push(p.b, k, p.y))
-        sib.append(push(p.b, k, p.sibling))
+    pass_over(p.b)
     yield
     on = []
     for k in early:
         to_x[k].wait_recv()
         on.append(push(p.b1, k, p.y))
-        sib.append(push(p.b1, k, p.sibling))
     for k in late:
         to_y[k].wait_recv()
         on.append(push(p.b2, k, p.x))
-        sib.append(push(p.b2, k, p.sibling))
     yield
     for k in late:
         to_x[k].wait_recv()
-        sib.append(push(p.b1, k, p.sibling))
+    pass_over(p.b1)
     for k in early:
         to_y[k].wait_recv()
-        sib.append(push(p.b2, k, p.sibling))
-    for k, copy in enumerate(on):
+    pass_over(p.b2)
+    for copy in on:
         copy.wait_recv()
-        sib.append(push(p.b3, k, p.sibling))
+    pass_over(p.b3)
     yield
     for copy in sib:
         copy.wait_recv()
 
 
 def fast_gather_copies(chips):
-    return chips - 1 + 3 * chips + 4 * chips
+    return chips - 1 + 3 * chips + 4
 
 
 def scatter_steps(place, copies, loads, grad, acc, got, near, far, last, result):
@@ -626,15 +627,11 @@
     meet(p)
     og_load = loads.start(og_hbm, og_ref)
     copies = Copies(send_sems, recv_sems)
-    half_down, half_pu = down_full.shape[3] // 2, pu_full.shape[4] // 2
     move = Schedule(
-        kv=fast_gather_steps(p, copies, qkv_full, cols=slice(width, 3 * width)),
+        qkv=fast_gather_steps(p, copies, qkv_full),
         norm=gather_steps(p, copies, norm_full),
-        q=gather_steps(p, copies, qkv_full, cols=slice(0, width)),
-        pu0=gather_steps(p, copies, pu_full, cols=slice(0, half_pu)),
-        pu1=gather_steps(p, copies, pu_full, cols=slice(half_pu, 2 * half_pu)),
-        down0=gather_steps(p, copies, down_full, rows=slice(0, half_down)),
-        down1=gather_steps(p, copies, down_full, rows=slice(half_down, 2 * half_down)),
+        pu=gather_steps(p, copies, pu_full),
+        down=gather_steps(p, copies, down_full),
     )
     xhat_ref = resid_ref
 
@@ -643,10 +640,9 @@
         x_load.wait(index)
         xhat_ref[here, :] = normalize(x_ref[here, :].astype(F32))[0]
 
-    move("norm", "kv")
-    loop(count, center, move.plan("norm kv q pu0", "", "norm kv", "norm kv q pu1"))
-    move("norm", "kv")
-    move("pu0")
+    move("norm", "qkv")
+    loop(count, center, move.plan("norm qkv pu", "", "norm qkv", "norm qkv"))
+    move("norm", "qkv", "pu")
     join_norms(norm_full, seqs, LANES // norm_ref.shape[1], norms_out)
     gain, shift = norms_out[0:1, :], norms_out[1:2, :]
 
@@ -666,15 +662,13 @@
                 mixed[part * SPAN : (part + 1) * SPAN], length, (first_span + span) * SPAN
             )
 
-    loop(count, keys_values, move.plan("q", "pu1 down0", "q"))
+    loop(count, keys_values)
     summ_ref[p.z, p.c] = sum_scr[...].astype(BF)
     along = [copies.push(summ_ref, (p.z, p.c), device) for device in p.along[1:]]
     sib = [copies.push(summ_ref, (p.z, p.c), p.sibling)]
-    move("down1", "pu0")
     for k, copy in enumerate(along, 1):
         copy.wait_recv()
         sib.append(copies.push(summ_ref, (p.before[k], p.c), p.sibling))
-    move("q")
     stores = [loads.start(qkv_full, qkv_hbm)]
     mixed_store = Sliced(loads, mixed_ref, mixed_hbm, count)
 
@@ -684,9 +678,9 @@
         mixed_store.start(index)
 
     loop(count, queries)
-    move("pu1")
     for copy in sib:
         copy.wait_recv()
+    move("pu")
     vt_scr[...] = summ_ref[:, :, :, width:].reshape(local * seqs, width).T
     summ_rows = SummaryView(summ_ref, local * seqs)
     attn_store = Sliced(loads, attn_ref, attn_hbm, count)
@@ -702,7 +696,7 @@
         attn_store.start(index)
         probs_store.start(index)
 
-    loop(count, attend, move.plan("pu0 down0", "pu1 down1", "pu0", "pu1"))
+    loop(count, attend, move.plan("down", "pu", "", "down pu"))
     gain_two, shift_two = norms_out[2:3, :], norms_out[3:4, :]
     resid_store, slope_store, activ_store = (
         Sliced(loads, src, dst, count)
@@ -724,7 +718,7 @@
         slope_store.start(index)
         activ_store.start(index)
 
-    loop(count, expand, move.plan("down0", "down1", "down0", "down1"))
+    loop(count, expand, move.plan("", "down", "", "down"))
     stores.append(loads.start(pu_full, pu_hbm))
     og_load.wait()
     parts = hidden // TILE
@@ -1261,7 +1255,7 @@
             vmem((rows, hidden), BF), vmem((rows, hidden), BF), vmem((hidden, width), BF),
             vmem((*grid3, 4, LANES), F32), vmem((local, 2 * width), F32), vmem((width, spans), BF),
         ],
-        4 + 7 * count + hidden // TILE, 6 * GATHER_COPIES + fast_gather_copies(chips) + 2 * chips,
+        4 + 7 * count + hidden // TILE, 3 * GATHER_COPIES + fast_gather_copies(chips) + 2 * chips,
     )(lengths, x, grad_rows, *state[:5])
     pu_flat, down_flat = pu_full.reshape(width, width + hidden), down_full.reshape(hidden, width)
     resid_grad, attn_grad, pu_grad, down_own, norm_two = remote_call(

time: 152 us -> 149 us (0.980)
  Pallas kernels: 150 us -> 147 us
    pallas_call x1, Pallas kernels: 66.4 us -> 63.4 us  [direct_body(): remote_call(front_kernel, groups, seqs, 'front', 0, [*((hbm, shape, BF) f...]
where the time goes in v3:
time: 149 us; the launch traced here: 148 us
  Pallas kernels  147 us (99%)
  between operations  1.49 us (1%)
    pallas_call x1, Pallas kernels, direct_body(): remote_call(front_kernel, groups, seqs, 'front', 0, [*((hbm, shape, BF) f...  63.4 us
    pallas_call x1, Pallas kernels, direct_body(): remote_call(back_kernel, groups, seqs, 'back', 2, [(hbm, tokens, BF), (hb...  50.6 us
    pallas_call x1, Pallas kernels, direct_body(): remote_call(middle_kernel, groups, seqs, 'middle', 1, [(hbm, tokens, F32)...  26.4 us
    pallas_call x1, Pallas kernels, body(): pl.pallas_call(functools.partial(update_kernel, parts), in_specs=[spec(vm...  6.6 us

profile of v3, /device:TPU:0, one launch (start us, length us, event | category | flops | bytes accessed | tf_op | source)
XLA Modules:
  0.0 148.5 jit_solution(11296837499840043161)
XLA Ops:
  1.3 63.4 %front.1 = (bf16[4,4,2,16,1536]{4,3,2,1,0:T(8,128)(2,1)}, bf16[4,4,2,16,2560]{4,3,2,1,0:T(8,128)(2,1)}, bf16[4,4,2,64,512]{4,3,2,1,0:T(8,128)(2,1)}, f32[4,512]{...) custom-call(s32[1]{0:T(128)S(6)} %copy.37.length_ref, ...), custom_call_target="tpu_custom_call" | custom-call | tf_op jit(solution)/shard_map/front/pallas_call | solution.py:1244
  64.7 26.4 %middle.1 = (f32[2048,512]{1,0:T(8,128)}, bf16[2048,512]{1,0:T(8,128)(2,1)}, bf16[512,2560]{1,0:T(8,128)(2,1)}, f32[64,512]{1,0:T(8,128)}, f32[2,512]{1,0:T(2,128)}) custom-call(bf16[2048,512]{1,0:T(8,128)(2,1)} %bitcast.17, f32[2048,512]{1,0:T(8,128)} %get-tuple-element.62.resid_hbm, bf16[2048,2048]{1,0:T(8,128)(2,1)} %get-tuple-element.63.slope_hbm, ...), custom_call_target="tpu_custom_call" | custom-call | tf_op jit(solution)/shard_map/middle/pallas_call | solution.py:1261
  91.1 50.6 %back.1 = (bf16[2048,512]{1,0:T(8,128)(2,1)}, bf16[2048,512]{1,0:T(8,128)(2,1)}, f32[16,1536]{1,0:T(8,128)}, f32[16,2560]{1,0:T(8,128)}, f32[4,512]{1,0:T(4,128)}, /*index=5*/f32[8,128]{1,0:T(8,128)}) custom-call(s32[1]{0:T(128)S(6)} %copy.37.length_ref, bf16[2048,512]{1,0:T(8,128)(2,1)} %bitcast.13, bf16[2048,1536]{1,0:T(8,128)(2,1)} %get-tuple-element.61.mixed_hbm, ...), custom_call_target="tpu_custom_call" | custom-call | tf_op jit(solution)/shard_map/back/pallas_call | solution.py:1292
  141.7 6.6 %update.1 = (bf16[2048,512]{1,0:T(8,128)(2,1)}, f32[2048,512]{1,0:T(8,128)}, f32[1,1]{1,0:T(1,128)}, f32[16,1536]{1,0:T(8,128)}, f32[16,512]{1,0:T(8,128)}, /*in...) custom-call(f32[8,128]{1,0:T(8,128)} %get-tuple-element.78.total_ref, ...), custom_call_target="tpu_custom_call" | custom-call | tf_op jit(solution)/shard_map/update/pallas_call | solution.py:1387

commit v4 on v3

--- a/solution.py
+++ b/solution.py
@@ -146,19 +146,20 @@
         dprobs = [dot_nt(v, g) for v, g in zip(values, grads)]
         scores = [mask_scores(s, unit[2]) for s, unit in zip(scores, units)]
         probs = [jnp.exp(s - lse_ref[index, pair : pair + 1, :]) for s, (_, index, _, pair) in zip(scores, units)]
+        lows = [p.astype(BF) for p in probs]
     else:
         dprobs = [dot_nt(v, g) for v, g in zip(values, grads)]
-        probs = []
+        lows = []
         for rows, _, _, pair in units:
             at = pair * 4 * SPAN
             near, far = probs_ref[rows, at : at + 2 * SPAN], probs_ref[rows, at + 2 * SPAN : at + 4 * SPAN]
-            probs.append(jnp.concatenate([near, far], axis=0).astype(F32))
+            lows.append(jnp.concatenate([near, far], axis=0))
+        probs = [low.astype(F32) for low in lows]
+    dvs = [dot(low, g) for low, g in zip(lows, grads)]
     deltas = [jnp.sum(p * d, axis=0, keepdims=True) for p, d in zip(probs, dprobs)]
     dscores = [(p * (d - delta)).astype(BF) for p, d, delta in zip(probs, dprobs, deltas)]
-    probs = [p.astype(BF) for p in probs]
     dqs = [dot(k, ds) for k, ds in zip(keys_t, dscores)]
     dks = [dot(ds, q) for ds, q in zip(dscores, queries)]
-    dvs = [dot(p, g) for p, g in zip(probs, grads)]
     for (rows, index, caps, pair), dq, dk, dv in zip(units, dqs, dks, dvs):
         at = pair * LANES
         back_ref[rows, at : at + LANES] = (fold_heads(dq) * 0.125).astype(BF)
@@ -560,8 +561,8 @@
 
 
 class Sliced:
-    def __init__(self, loads, src, dst, count):
-        self.src, self.dst, self.count, self.size = src, dst, count, src.shape[0] // count
+    def __init__(self, loads, src, dst, count, dim=0):
+        self.src, self.dst, self.count, self.size, self.dim = src, dst, count, src.shape[dim] // count, dim
         self.sems, self.first = loads.sems, loads.made
         loads.made += count
         assert loads.made <= loads.sems.shape[0]
@@ -569,7 +570,8 @@
     def copy(self, index):
         begin = index * self.size
         here = pl.ds(begin if isinstance(index, int) else pl.multiple_of(begin, self.size), self.size)
-        return pltpu.make_async_copy(self.src.at[here], self.dst.at[here], self.sems.at[self.first + index])
+        where = (slice(None),) * self.dim + (here,)
+        return pltpu.make_async_copy(self.src.at[where], self.dst.at[where], self.sems.at[self.first + index])
 
     def start(self, index):
         self.copy(index).start()
@@ -814,18 +816,22 @@
 
     loop(count, tile, move.plan("down0", "down1", "down0", "down1 down0"))
     attn_load.wait()
+    pu_store = Sliced(loads, pu_grad_ref, pu_grad_hbm, (width + hidden) // TILE, dim=1)
+    proj = width // TILE
     pu_grad_ref[:, :width] = dot_tn(attn_ref[...], pig_ref[...]).astype(BF)
+    for index in range(proj):
+        pu_store.start(index)
 
     def up_grad(index):
-        at = pl.multiple_of(width + index * TILE, TILE)
-        pu_grad_ref[:, pl.ds(at, TILE)] = dot_tn(normed_ref[...], pre_grad_ref[:, row_block(index, TILE)]).astype(BF)
+        here = row_block(index + proj, TILE)
+        pu_grad_ref[:, here] = dot_tn(normed_ref[...], pre_grad_ref[:, row_block(index, TILE)]).astype(BF)
+        pu_store.start(index + proj)
 
     loop(hidden // TILE, up_grad, move.plan("down1", "", "down0"))
-    pu_store = loads.start(pu_grad_ref, pu_grad_hbm)
     resid_grad_store.wait_all()
     attn_grad_store.wait_all()
     move.finish()
-    pu_store.wait()
+    pu_store.wait_all()
     copies.finish()
 
 
@@ -1271,7 +1277,7 @@
             vmem(pu_flat.shape, BF), vmem((rows, hidden), BF), vmem(tokens, BF), vmem(tokens, BF),
             *scatter_scratch(groups, chips, down_rows // 2, width) * 2,
         ],
-        6 + 5 * count, 2 * SCATTER_COPIES,
+        6 + 5 * count + (width + hidden) // TILE, 2 * SCATTER_COPIES,
     )(grad_rows, resid, slope, attn_out, pu_flat, down_flat, norms, down_grad.reshape(shapes[2]))
     half = (width + hidden) // 2
     blocks = ((own_rows, half),) * 2 + ((own_rows, width),) * 3

time: 149 us -> 147 us (0.987)
  no operation moved by 1% of the time
where the time goes in v4:
time: 147 us
  Pallas kernels  146 us (99%)
  between operations  1.49 us (1%)
    pallas_call x1, Pallas kernels, direct_body(): remote_call(front_kernel, groups, seqs, 'front', 0, [*((hbm, shape, BF) f...  63.4 us
    pallas_call x1, Pallas kernels, direct_body(): remote_call(back_kernel, groups, seqs, 'back', 2, [(hbm, tokens, BF), (hb...  49.8 us
    pallas_call x1, Pallas kernels, direct_body(): remote_call(middle_kernel, groups, seqs, 'middle', 1, [(hbm, tokens, F32)...  25.8 us
    pallas_call x1, Pallas kernels, body(): pl.pallas_call(functools.partial(update_kernel, parts), in_specs=[spec(vm...  6.6 us

profile of v4, /device:TPU:0, one launch (start us, length us, event | category | flops | bytes accessed | tf_op | source)
XLA Modules:
  0.0 147.1 jit_solution(8585619466371932473)
XLA Ops:
  1.3 63.4 %front.1 = (bf16[4,4,2,16,1536]{4,3,2,1,0:T(8,128)(2,1)}, bf16[4,4,2,16,2560]{4,3,2,1,0:T(8,128)(2,1)}, bf16[4,4,2,64,512]{4,3,2,1,0:T(8,128)(2,1)}, f32[4,512]{...) custom-call(s32[1]{0:T(128)S(6)} %copy.37.length_ref, ...), custom_call_target="tpu_custom_call" | custom-call | tf_op jit(solution)/shard_map/front/pallas_call | solution.py:1250
  64.7 25.8 %middle.1 = (f32[2048,512]{1,0:T(8,128)}, bf16[2048,512]{1,0:T(8,128)(2,1)}, bf16[512,2560]{1,0:T(8,128)(2,1)}, f32[64,512]{1,0:T(8,128)}, f32[2,512]{1,0:T(2,128)}) custom-call(bf16[2048,512]{1,0:T(8,128)(2,1)} %bitcast.17, f32[2048,512]{1,0:T(8,128)} %get-tuple-element.62.resid_hbm, bf16[2048,2048]{1,0:T(8,128)(2,1)} %get-tuple-element.63.slope_hbm, ...), custom_call_target="tpu_custom_call" | custom-call | tf_op jit(solution)/shard_map/middle/pallas_call | solution.py:1267
  90.5 49.8 %back.1 = (bf16[2048,512]{1,0:T(8,128)(2,1)}, bf16[2048,512]{1,0:T(8,128)(2,1)}, f32[16,1536]{1,0:T(8,128)}, f32[16,2560]{1,0:T(8,128)}, f32[4,512]{1,0:T(4,128)}, /*index=5*/f32[8,128]{1,0:T(8,128)}) custom-call(s32[1]{0:T(128)S(6)} %copy.37.length_ref, bf16[2048,512]{1,0:T(8,128)(2,1)} %bitcast.13, bf16[2048,1536]{1,0:T(8,128)(2,1)} %get-tuple-element.61.mixed_hbm, ...), custom_call_target="tpu_custom_call" | custom-call | tf_op jit(solution)/shard_map/back/pallas_call | solution.py:1298
  140.3 6.6 %update.1 = (bf16[2048,512]{1,0:T(8,128)(2,1)}, f32[2048,512]{1,0:T(8,128)}, f32[1,1]{1,0:T(1,128)}, f32[16,1536]{1,0:T(8,128)}, f32[16,512]{1,0:T(8,128)}, /*in...) custom-call(f32[8,128]{1,0:T(8,128)} %get-tuple-element.78.total_ref, ...), custom_call_target="tpu_custom_call" | custom-call | tf_op jit(solution)/shard_map/update/pallas_call | solution.py:1393
